TPU v7x, 128 devices: a whole 4x4x4 slice. The times are simulated.
128 devices in a mesh: grp: 8 (over x, core), rep: 16 (over y, z).
Axes of the slice: x: 4, y: 4, z: 4, core: 2. Of those that a mesh axis runs over, the one named last changes fastest.
Arguments:
- item_table: bfloat16 [524288, 256], P(('grp', 'rep')), may hold values from -6 to 6
- send_rows: int32 [128, 128, 32], P(('grp', 'rep')), may hold values from 0 to 4095, as said below
- send_count: int32 [128, 128], P(('grp', 'rep')), may hold values from 24 to 32, as said below
- pos_slot: int32 [131072], P(('grp', 'rep')), may hold values from 0 to 4095, as said below
- neg_slot: int32 [128, 1024], P(('grp', 'rep')), may hold values from 0 to 4095, as said below
- user_ids: int32 [131072, 8], P(('grp', 'rep')), may hold values from 0 to 8191
- user_table: bfloat16 [8192, 256], replicated, may hold values from -2.09375 to 2.09375
- item_w1: bfloat16 [256, 512], replicated, may hold values from -0.375 to 0.375
- item_w2: bfloat16 [512, 128], replicated, may hold values from -0.25 to 0.25
- user_w1: bfloat16 [256, 512], replicated, may hold values from -0.375 to 0.375
- user_w2: bfloat16 [512, 128], replicated, may hold values from -0.25 to 0.25
Outputs:
- table_grad: float32 [524288, 256], P(('grp', 'rep'))
- example_loss: float32 [131072], P(('grp', 'rep'))
Inputs may be any that keep to these rules, and one draw needn't show every extreme that they name: `send_rows`: within one list (one owner, one batch owner) the 32 entries are distinct local row numbers; entries at or beyond the list's count are unused. `send_count`: some batch owner receives 32 rows from every owner. `pos_slot`: each entry names a used slot, source * 32 + j with j below that list's count, of its batch owner's receive buffer. `neg_slot`: each entry names a used slot of its batch owner's receive buffer, numbered as for pos_slot.
All inputs are finite; a program needn't handle non-finite values.
Results may differ from a plain program's by a relative error of at most 0.02.
Values may be sent and summed in bfloat16 or wider, within the bound.
A program may use at most 128 MiB of HBM per device.

v0:
```python
import jax
import jax.numpy as jnp
from jax import lax
from jax.sharding import PartitionSpec as P

LOGIT_SCALE = 20.0
NORM_EPS = 1e-06


def tower(inputs, first_w, second_w):
    preact = jnp.dot(inputs, first_w, preferred_element_type=jnp.float32)
    hidden = jax.nn.silu(preact).astype(jnp.bfloat16)
    output = jnp.dot(hidden, second_w, preferred_element_type=jnp.float32)
    length = jnp.sqrt(jnp.sum(output * output, axis=-1, keepdims=True) + NORM_EPS)
    return (preact, length, output / length)


def per_device(
    item_table,
    send_rows,
    send_count,
    pos_slot,
    neg_slot,
    user_ids,
    user_table,
    item_w1,
    item_w2,
    user_w1,
    user_w2,
):
    peer_count = lax.axis_size(("grp", "rep"))
    cap_slots = send_rows.shape[2]
    emb_width = item_table.shape[1]
    batch_rows = pos_slot.shape[0]
    row_ids = send_rows[0]
    live_mask = jnp.arange(cap_slots, dtype=jnp.int32)[None, :] < send_count[0][:, None]
    outgoing = item_table[row_ids] * live_mask[..., None].astype(jnp.bfloat16)
    arrived = lax.all_to_all(outgoing, ("grp", "rep"), split_axis=0, concat_axis=0, tiled=True)
    item_rows = arrived.reshape(peer_count * cap_slots, emb_width)
    preact, length, unit = tower(item_rows, item_w1, item_w2)
    item_vec = unit.astype(jnp.bfloat16)
    positive = item_vec[pos_slot]
    negative = item_vec[neg_slot[0]]
    pooled = jnp.sum(user_table[user_ids].astype(jnp.float32), axis=1).astype(jnp.bfloat16)
    queries = tower(pooled, user_w1, user_w2)[2].astype(jnp.bfloat16)
    pos_scores = LOGIT_SCALE * jnp.einsum(
        "bo,co->bc",
        queries,
        lax.all_gather(positive, "grp", axis=0, tiled=True),
        preferred_element_type=jnp.float32,
    )
    neg_scores = LOGIT_SCALE * jnp.einsum(
        "bo,co->bc", queries, negative, preferred_element_type=jnp.float32
    )
    log_total = jnp.log(jnp.sum(jnp.exp(pos_scores), axis=1) + jnp.sum(jnp.exp(neg_scores), axis=1))
    label_cols = lax.axis_index("grp") * batch_rows + jnp.arange(batch_rows, dtype=jnp.int32)
    picked = jnp.take_along_axis(pos_scores, label_cols[:, None], axis=1)[:, 0]
    example_loss = log_total - picked
    slope_neg = (LOGIT_SCALE * jnp.exp(neg_scores - log_total[:, None])).astype(jnp.bfloat16)
    neg_grad = jnp.einsum("bc,bo->co", slope_neg, queries, preferred_element_type=jnp.float32)
    onehot = (
        jnp.arange(pos_scores.shape[1], dtype=jnp.int32)[None, :] == label_cols[:, None]
    ).astype(jnp.float32)
    slope_pos = (LOGIT_SCALE * (jnp.exp(pos_scores - log_total[:, None]) - onehot)).astype(
        jnp.bfloat16
    )
    pos_grad = lax.psum_scatter(
        jnp.einsum("bc,bo->co", slope_pos, queries, preferred_element_type=jnp.float32).astype(
            jnp.bfloat16
        ),
        "grp",
        scatter_dimension=0,
        tiled=True,
    ).astype(jnp.float32)
    slot_grads = jnp.zeros((peer_count * cap_slots, unit.shape[1]), jnp.float32)
    slot_grads = slot_grads.at[pos_slot].add(pos_grad).at[neg_slot[0]].add(neg_grad)
    radial = jnp.sum(unit * slot_grads, axis=-1, keepdims=True)
    d_output = ((slot_grads - unit * radial) / length).astype(jnp.bfloat16)
    d_hidden = jnp.einsum("so,ho->sh", d_output, item_w2, preferred_element_type=jnp.float32)
    sigmoid_pre = jax.nn.sigmoid(preact)
    d_pre = (d_hidden * sigmoid_pre * (1.0 + preact * (1.0 - sigmoid_pre))).astype(jnp.bfloat16)
    d_items = jnp.einsum("sh,eh->se", d_pre, item_w1, preferred_element_type=jnp.float32).astype(
        jnp.bfloat16
    )
    returned = lax.all_to_all(
        d_items.reshape(peer_count, cap_slots, emb_width),
        ("grp", "rep"),
        split_axis=0,
        concat_axis=0,
        tiled=True,
    )
    values = returned.astype(jnp.float32) * live_mask[..., None].astype(jnp.float32)
    table_grad = jnp.zeros((item_table.shape[0], emb_width), jnp.float32)
    table_grad = table_grad.at[row_ids.reshape(-1)].add(values.reshape(-1, emb_width))
    return (table_grad, example_loss)


def solution(mesh):
    return jax.shard_map(
        per_device,
        mesh=mesh,
        in_specs=(
            P(("grp", "rep"), None),
            P(("grp", "rep"), None, None),
            P(("grp", "rep"), None),
            P(("grp", "rep")),
            P(("grp", "rep"), None),
            P(("grp", "rep"), None),
            P(),
            P(),
            P(),
            P(),
            P(),
        ),
        out_specs=(P(("grp", "rep"), None), P(("grp", "rep"))),
        check_vma=False,
    )
```

profile of v0, /device:TPU:1, one launch (start us, length us, event | category | flops | bytes accessed | tf_op | source)
XLA Modules:
  0.0 307.6 jit_solution(6599303792608771970)
XLA Ops:
  9.0 17.0 %gather_fusion.1 = bf16[4096,256]{1,0:T(8,128)(2,1)} fusion(bf16[4096,256]{1,0:T(8,128)(2,1)S(1)} %copy-done, s32[4096]{0:T(1024)S(1)} %broadcast_clamp_fusion.1), kind=kCustom, calls=%fused_computation.1 | custom fusion | bytes 4210688 | tf_op jit(solution)/shard_map/gather | solution.py:37
  26.0 2.9 broadcast_multiply_fusion.1
  29.0 11.5 %all-to-all-start = ((bf16[128,32,256]{2,1,0:T(8,128)(2,1)}), bf16[128,32,256]{2,1,0:T(8,128)(2,1)S(1)}, u32[]{:S(2)}, u32[]{:S(2)}) async-start(bf16[128,32,256]{2,1,0:T(8,128)(2,1)} %broadcast_multiply_fusion.1), calls=%async_computation | async-start | bytes 4194304 | tf_op jit(solution)/shard_map/all_to_all | solution.py:38
  40.6 29.4 %all-to-all-done = bf16[128,32,256]{2,1,0:T(8,128)(2,1)S(1)} async-done(((bf16[128,32,256]{2,1,0:T(8,128)(2,1)}), bf16[128,32,256]{2,1,0:T(8,128)(2,1)S(1)}, u32[]{:S(2)}, u32[]{:S(2)}) %all-to-all-start) | async-done | bytes 2097184 | tf_op jit(solution)/shard_map/all_to_all | solution.py:38
  71.2 3.2 %multiply_reduce_fusion.1 = (f32[4096]{0:T(1024)S(1)}, f32[4096,128]{0,1:T(8,128)S(1)}) fusion(bf16[512,128]{1,0:T(8,128)(2,1)S(1)} %copy-done.12, f32[4096,512]{1,0:T(8,128)S(1)} %fusion.26), kind=kOutput, calls=%fused_computation.25 | convolution fusion | flops 548401152 | bytes 10633216 | tf_op jit(solution)/shard_map/dot_general | solution.py:13
  76.6 4.3 %gather_fusion.2 = bf16[1024,128]{1,0:T(8,128)(2,1)} fusion(bf16[4096,128]{1,0:T(8,128)(2,1)S(1)} %copy.20, s32[1024]{0:T(1024)S(1)} %get-tuple-element.4), kind=kCustom, calls=%fused_computation.2 | custom fusion | bytes 528384 | tf_op jit(solution)/shard_map/gather | solution.py:42
  81.5 34.1 %gather_fusion = bf16[8192,256]{1,0:T(8,128)(2,1)} fusion(bf16[8192,256]{1,0:T(8,128)(2,1)} %param.17, s32[8192]{0:T(1024)S(1)} %broadcast_clamp_fusion), kind=kCustom, calls=%fused_computation | custom fusion | bytes 8421376 | tf_op jit(solution)/shard_map/gather | solution.py:44
  115.6 5.0 %bitcast_reduce_fusion = bf16[1024,256]{1,0:T(8,128)(2,1)S(1)} fusion(bf16[8192,256]{1,0:T(8,128)(2,1)} %gather_fusion), kind=kLoop, calls=%fused_computation.18 | loop fusion | flops 1835008 | bytes 4718592 | tf_op jit(solution)/shard_map/reduce_sum | solution.py:44
  121.7 3.2 %gather_fusion.3 = bf16[1024,128]{1,0:T(8,128)(2,1)S(1)} fusion(bf16[4096,128]{1,0:T(8,128)(2,1)S(1)} %copy.20, s32[1024]{0:T(1024)S(1)} %broadcast_clamp_fusion.2), kind=kCustom, calls=%fused_computation.3 | custom fusion | bytes 528384 | tf_op jit(solution)/shard_map/gather | solution.py:43
  124.9 2.7 exponential_reduce_fusion.1
  127.7 15.0 %exponential_reduce_fusion = (f32[1024]{0:T(1024)S(1)}, f32[1024,8192]{1,0:T(8,128)}) fusion(bf16[1024,128]{0,1:T(8,128)(2,1)S(1)} %divide_convert_fusion.3, bf16[8192,128]{1,0:T(8,128)(2,1)} %all-gather.3.cloned.1.call-done), kind=kOutput, calls=%fused_computation.10 | convolution fusion | flops 2164259840 | bytes 35917824 | tf_op jit(solution)/shard_map/bo,co->bc/dot_general | solution.py:46
  142.7 17.4 %gather_fusion.4 = f32[1024]{0:T(1024)S(1)} fusion(f32[1024,8192]{1,0:T(8,128)} %get-tuple-element.13, s32[1024]{0:T(1024)S(1)} %bitcast.32), kind=kCustom, calls=%fused_computation.4 | custom fusion | bytes 16384 | tf_op jit(solution)/shard_map/jit(take_along_axis)/gather | solution.py:57
  160.8 18.1 %fusion.1 = bf16[8192,128]{1,0:T(8,128)(2,1)} fusion(bf16[1024,128]{0,1:T(8,128)(2,1)S(1)} %divide_convert_fusion.3, f32[1024,8192]{1,0:T(8,128)} %get-tuple-element.13, s32[1024]{0:T(1024)S(1)} %iota_add_fusion, f32[1024]{0:T(1024)S(1)} %get-tuple-element.3), kind=kOutput, calls=%fused_computation.13 | convolution fusion | flops 2198863872 | bytes 35921920 | tf_op jit(solution)/shard_map/bc,bo->co/dot_general | solution.py:68
  178.9 3.1 %fusion.5 = f32[1024,128]{1,0:T(8,128)S(1)} fusion(bf16[1024,128]{0,1:T(8,128)(2,1)S(1)} %divide_convert_fusion.3, f32[1024,1024]{0,1:T(8,128)} %get-tuple-element.15, f32[1024]{0:T(1024)S(1)} %get-tuple-element.3), kind=kOutput, calls=%fused_computation.29 | convolution fusion | flops 272629760 | bytes 4984832 | tf_op jit(solution)/shard_map/bc,bo->co/dot_general | solution.py:60
  182.0 24.1 %reduce-scatter.2.cloned.1.call-done = bf16[1024,128]{1,0:T(8,128)(2,1)} async-done(((bf16[8192,128]{1,0:T(8,128)(2,1)}), bf16[1024,128]{1,0:T(8,128)(2,1)}) %reduce-scatter.2.cloned.1.call-update) | async-done | bytes 262160 | tf_op jit(solution)/shard_map/reduce_scatter | solution.py:67
  206.1 6.9 %scatter_custom_fusion = f32[4096,128]{1,0:T(8,128)S(1)} fusion(s32[1024]{0:T(1024)S(1)} %get-tuple-element.5, f32[]{:T(128)} %constant.13.clone.1, bf16[1024,128]{1,0:T(8,128)(2,1)} %reduce-scatter.2.cloned.1.call-done), kind=kCustom, calls=%fused_computation.36 | custom fusion | flops 262144 | bytes 2359300 | tf_op jit(solution)/shard_map/scatter-add | solution.py:76
  213.1 6.8 %scatter_fusion = f32[4096,128]{1,0:T(8,128)S(1)} fusion(f32[4096,128]{1,0:T(8,128)S(1)} %scatter_custom_fusion, s32[1024]{0:T(1024)S(1)} %bitcast.38, f32[1024,128]{1,0:T(8,128)S(1)} %fusion.5), kind=kCustom, calls=%fused_computation.6 | custom fusion | flops 131072 | bytes 1576960 | tf_op jit(solution)/shard_map/scatter-add | solution.py:76
  219.9 1.8 copy.23
  221.7 2.7 multiply_reduce_fusion
  224.5 7.8 %convolution_convert_fusion = bf16[4096,256]{1,0:T(8,128)(2,1)} fusion(bf16[256,512]{1,0:T(8,128)(2,1)S(1)} %copy-done.5, f32[4096,512]{1,0:T(8,128)} %copy-done.2, bf16[512,128]{1,0:T(8,128)(2,1)S(1)} %copy-done.13, f32[4096,128]{0,1:T(8,128)} %copy.23, f32[4096]{0:T(1024)S(1)} %multiply_reduce_fusion, f32[4096]{0:T(1024)S(1)} %add_sqrt_fusion, ...), kind=kOutput, calls=%fused_computation.17 | convolution fusion | flops 1633157120 | bytes 15106048 | tf_op jit(solution)/shard_map/sh,eh->se/dot_general | solution.py:82
  232.3 10.5 %all-to-all-start.1 = ((bf16[128,32,256]{2,1,0:T(8,128)(2,1)}), bf16[128,32,256]{2,1,0:T(8,128)(2,1)}, u32[]{:S(2)}, u32[]{:S(2)}) async-start(bf16[128,32,256]{2,1,0:T(8,128)(2,1)} %bitcast.36), calls=%async_computation.2 | async-start | bytes 4194304 | tf_op jit(solution)/shard_map/all_to_all | solution.py:85
  243.1 28.9 %all-to-all-done.1 = bf16[128,32,256]{2,1,0:T(8,128)(2,1)} async-done(((bf16[128,32,256]{2,1,0:T(8,128)(2,1)}), bf16[128,32,256]{2,1,0:T(8,128)(2,1)}, u32[]{:S(2)}, u32[]{:S(2)}) %all-to-all-start.1) | async-done | bytes 2097184 | tf_op jit(solution)/shard_map/all_to_all | solution.py:85
  272.0 3.6 %convert_multiply_fusion = f32[128,32,256]{2,1,0:T(8,128)} fusion(bf16[128,32,256]{2,1,0:T(8,128)(2,1)} %all-to-all-done.1, f32[128,32]{1,0:T(8,128)S(1)} %get-tuple-element.6), kind=kLoop, calls=%fused_computation.19 | loop fusion | flops 2097152 | bytes 6307840 | tf_op jit(solution)/shard_map/mul | solution.py:92
  275.7 25.1 %scatter_custom_fusion.2 = f32[4096,256]{1,0:T(8,128)} fusion(s32[4096]{0:T(1024)S(1)} %bitcast.39, f32[4096,256]{1,0:T(8,128)} %bitcast.35, f32[]{:T(128)} %constant.13.clone.1), kind=kCustom, calls=%fused_computation.27 | custom fusion | flops 1048576 | bytes 4194816 | tf_op jit(solution)/shard_map/scatter-add | solution.py:94
  (61 shorter events, 7.8 us)
Async XLA Ops:
  7.2 1.8 copy-start
  26.0 14.5 %copy-start.8 = (s32[1024]{0:T(1024)S(1)}, s32[1024]{0:T(1024)}, u32[]{:S(2)}) copy-start(s32[1024]{0:T(1024)} %param.14) | copy-start | bytes 12292
  26.0 43.9 %copy-start.5 = (bf16[256,512]{1,0:T(8,128)(2,1)S(1)}, bf16[256,512]{1,0:T(8,128)(2,1)}, u32[]{:S(2)}) copy-start(bf16[256,512]{1,0:T(8,128)(2,1)} %param.18) | copy-start | bytes 786436
  29.0 41.0 %all-to-all-start = ((bf16[128,32,256]{2,1,0:T(8,128)(2,1)}), bf16[128,32,256]{2,1,0:T(8,128)(2,1)S(1)}, u32[]{:S(2)}, u32[]{:S(2)}) async-start(bf16[128,32,256]{2,1,0:T(8,128)(2,1)} %broadcast_multiply_fusion.1), calls=%async_computation | async-start | bytes 4194304 | tf_op jit(solution)/shard_map/all_to_all | solution.py:38
  40.5 87.2 %all-gather.3.cloned.1.call-start = ((), (), s32[]{:S(2)}) async-start(), calls=%async_computation.4 | async-start | bytes 2359296 | tf_op jit(solution)/shard_map/all_gather | solution.py:49
  70.0 1.3 copy-start.12
  71.2 3.2 %copy-start.2 = (f32[4096,512]{1,0:T(8,128)}, f32[4096,512]{1,0:T(8,128)S(1)}, u32[]{:S(2)}) copy-start(f32[4096,512]{1,0:T(8,128)S(1)} %fusion.26) | copy-start | bytes 25165828
  74.5 1.3 copy-start.3
  74.5 6.5 %copy-start.7 = (s32[1024,8]{0,1:T(8,128)S(1)}, s32[1024,8]{0,1:T(8,128)}, u32[]{:S(2)}) copy-start(s32[1024,8]{0,1:T(8,128)} %param.16) | copy-start | bytes 98308
  80.9 125.2 %reduce-scatter.2.cloned.1.call-start = ((), (), s32[]{:S(2)}) async-start(), calls=%async_computation.3 | async-start | bytes 2359296 | tf_op jit(solution)/shard_map/reduce_scatter | solution.py:67
  115.6 5.1 %copy-start.10 = (bf16[256,512]{1,0:T(8,128)(2,1)S(1)}, bf16[256,512]{1,0:T(8,128)(2,1)}, u32[]{:S(2)}) copy-start(bf16[256,512]{1,0:T(8,128)(2,1)} %param.20) | copy-start | bytes 786436
  115.6 5.1 %copy-start.11 = (bf16[512,128]{1,0:T(8,128)(2,1)S(1)}, bf16[512,128]{1,0:T(8,128)(2,1)}, u32[]{:S(2)}) copy-start(bf16[512,128]{1,0:T(8,128)(2,1)} %param.21) | copy-start | bytes 393220
  120.7 0.9 copy-start.9
  219.9 4.5 %copy-start.13 = (bf16[512,128]{1,0:T(8,128)(2,1)S(1)}, bf16[512,128]{1,0:T(8,128)(2,1)}, u32[]{:S(2)}) copy-start(bf16[512,128]{1,0:T(8,128)(2,1)} %param.19) | copy-start | bytes 393220
  221.7 2.9 copy-start.4
  232.3 10.6 %copy-start.6 = (s32[1,128,32]{1,2,0:T(8,128)S(1)}, s32[1,128,32]{1,2,0:T(8,128)}, u32[]{:S(2)}) copy-start(s32[1,128,32]{1,2,0:T(8,128)} %param.12) | copy-start | bytes 49156
  232.3 39.7 %all-to-all-start.1 = ((bf16[128,32,256]{2,1,0:T(8,128)(2,1)}), bf16[128,32,256]{2,1,0:T(8,128)(2,1)}, u32[]{:S(2)}, u32[]{:S(2)}) async-start(bf16[128,32,256]{2,1,0:T(8,128)(2,1)} %bitcast.36), calls=%async_computation.2 | async-start | bytes 4194304 | tf_op jit(solution)/shard_map/all_to_all | solution.py:85
  272.0 28.7 %copy-start.1 = (bf16[4096,256]{1,0:T(8,128)(2,1)S(1)}, bf16[4096,256]{1,0:T(8,128)(2,1)}, u32[]{:S(2)}) copy-start(bf16[4096,256]{1,0:T(8,128)(2,1)} %param.11) | copy-start | bytes 6291460
Sparse Core Ops, SparseCore 0:
  81.1 22.1 all-gather.2
  179.0 27.0 reduce-scatter.1
where the time goes:
time: 309 us; the launch traced here: 308 us
  waiting for transfers between devices  82.5 us (27%)
  local copies, waits for them, and re-layouts  80.9 us (26%)
  other arithmetic  55.6 us (18%)
  matrix products  52.1 us (17%)
  starting transfers between devices  22.1 us (7%)
  between operations  14.4 us (5%)
    gather x1, local copies, waits for them, and re-layouts, per_device(): user_table[user_ids].astype(jnp.float32)  34.1 us
    all_to_all x1, waiting for transfers between devices, per_device(): lax.all_to_all(outgoing, ('grp', 'rep'), split_axis=0, concat_axis=0, til...  29.4 us
    all_to_all x1, waiting for transfers between devices, per_device(): lax.all_to_all(d_items.reshape(peer_count, cap_slots, emb_width), ('grp',...  28.9 us
    scatter-add x1, other arithmetic, per_device(): table_grad.at[row_ids.reshape(-1)].add(values.reshape(-1, emb_width))  25.1 us
    reduce_scatter x1, waiting for transfers between devices, per_device(): lax.psum_scatter(jnp.einsum('bc,bo->co', slope_pos, queries, preferred_el...  24.1 us
    dot_general x1, matrix products, per_device(): jnp.einsum('bc,bo->co', slope_pos, queries, preferred_element_type=jnp.fl...  18.1 us
    gather x1, local copies, waits for them, and re-layouts, per_device(): picked = jnp.take_along_axis(pos_scores, label_cols[:, None], axis=1)[:, 0]  17.4 us
    gather x1, local copies, waits for them, and re-layouts, per_device(): outgoing = item_table[row_ids] * live_mask[..., None].astype(jnp.bfloat16)  17 us
  transfers between devices with their start and end apart: 4, of which 3 were waited for; matrix products, arithmetic and copies ran while one was open for 16% of the time, Pallas kernels for 0%

commit v1 on v0

v1 whole, which is shorter than its diff:
```python
import jax
import jax.numpy as jnp
from jax import lax
from jax.sharding import PartitionSpec as P

LOGIT_SCALE = 20.0
NORM_EPS = 1e-06


def tower(inputs, first_w, second_w):
    preact = jnp.dot(inputs, first_w, preferred_element_type=jnp.float32)
    hidden = jax.nn.silu(preact).astype(jnp.bfloat16)
    output = jnp.dot(hidden, second_w, preferred_element_type=jnp.float32)
    length = jnp.sqrt(jnp.sum(output * output, axis=-1, keepdims=True) + NORM_EPS)
    return (preact, length, output / length)


def per_device(
    item_table,
    send_rows,
    send_count,
    pos_slot,
    neg_slot,
    user_ids,
    user_table,
    item_w1,
    item_w2,
    user_w1,
    user_w2,
):
    peer_count = lax.axis_size(("grp", "rep"))
    cap_slots = send_rows.shape[2]
    batch_rows = pos_slot.shape[0]
    row_ids = send_rows[0]
    live_mask = jnp.arange(cap_slots, dtype=jnp.int32)[None, :] < send_count[0][:, None]

    pooled = jnp.sum(user_table[user_ids].astype(jnp.float32), axis=1).astype(jnp.bfloat16)
    queries = tower(pooled, user_w1, user_w2)[2].astype(jnp.bfloat16)
    group_queries = lax.all_gather(queries, "grp", axis=0, tiled=True)

    preact, length, unit = tower(item_table, item_w1, item_w2)
    item_vec = unit.astype(jnp.bfloat16)
    outgoing = item_vec[row_ids] * live_mask[..., None].astype(jnp.bfloat16)
    arrived = lax.all_to_all(outgoing, ("grp", "rep"), split_axis=0, concat_axis=0, tiled=True)
    slot_vec = arrived.reshape(peer_count * cap_slots, -1)
    positive = slot_vec[pos_slot]
    negative = slot_vec[neg_slot[0]]

    neg_exp = jnp.exp(
        LOGIT_SCALE
        * jnp.einsum("bo,co->bc", queries, negative, preferred_element_type=jnp.float32)
    )
    user_at = jnp.arange(group_queries.shape[0], dtype=jnp.int32)[:, None]
    own_at = lax.axis_index("grp") * batch_rows + jnp.arange(batch_rows, dtype=jnp.int32)[None, :]
    pos_exp = jnp.where(
        user_at == own_at,
        0.0,
        jnp.exp(
            LOGIT_SCALE
            * jnp.einsum("bo,co->bc", group_queries, positive, preferred_element_type=jnp.float32)
        ),
    )
    other_sum = lax.psum_scatter(
        jnp.sum(pos_exp, axis=1), "grp", scatter_dimension=0, tiled=True
    ) + jnp.sum(neg_exp, axis=1)
    own_score = LOGIT_SCALE * jnp.sum(
        queries.astype(jnp.float32) * positive.astype(jnp.float32), axis=1
    )
    total = other_sum + jnp.exp(own_score)
    example_loss = jnp.log(total) - own_score
    rate = LOGIT_SCALE / total
    group_rate = lax.all_gather(rate, "grp", axis=0, tiled=True)

    neg_grad = jnp.einsum(
        "bc,bo->co",
        neg_exp.astype(jnp.bfloat16),
        (queries.astype(jnp.float32) * rate[:, None]).astype(jnp.bfloat16),
        preferred_element_type=jnp.float32,
    )
    pos_grad = jnp.einsum(
        "bc,bo->co",
        pos_exp.astype(jnp.bfloat16),
        (group_queries.astype(jnp.float32) * group_rate[:, None]).astype(jnp.bfloat16),
        preferred_element_type=jnp.float32,
    ) - (rate * other_sum)[:, None] * queries.astype(jnp.float32)

    slot_grads = jnp.zeros((peer_count * cap_slots, unit.shape[1]), jnp.float32)
    slot_grads = slot_grads.at[pos_slot].add(pos_grad).at[neg_slot[0]].add(neg_grad)
    returned = lax.all_to_all(
        slot_grads.astype(jnp.bfloat16).reshape(peer_count, cap_slots, -1),
        ("grp", "rep"),
        split_axis=0,
        concat_axis=0,
        tiled=True,
    )
    values = returned.astype(jnp.float32) * live_mask[..., None].astype(jnp.float32)
    row_grads = jnp.zeros(unit.shape, jnp.float32)
    row_grads = row_grads.at[row_ids.reshape(-1)].add(values.reshape(-1, unit.shape[1]))

    radial = jnp.sum(unit * row_grads, axis=-1, keepdims=True)
    d_output = ((row_grads - unit * radial) / length).astype(jnp.bfloat16)
    d_hidden = jnp.einsum("so,ho->sh", d_output, item_w2, preferred_element_type=jnp.float32)
    sigmoid_pre = jax.nn.sigmoid(preact)
    d_pre = (d_hidden * sigmoid_pre * (1.0 + preact * (1.0 - sigmoid_pre))).astype(jnp.bfloat16)
    table_grad = jnp.einsum("sh,eh->se", d_pre, item_w1, preferred_element_type=jnp.float32)
    return (table_grad, example_loss)


def solution(mesh):
    return jax.shard_map(
        per_device,
        mesh=mesh,
        in_specs=(
            P(("grp", "rep"), None),
            P(("grp", "rep"), None, None),
            P(("grp", "rep"), None),
            P(("grp", "rep")),
            P(("grp", "rep"), None),
            P(("grp", "rep"), None),
            P(),
            P(),
            P(),
            P(),
            P(),
        ),
        out_specs=(P(("grp", "rep"), None), P(("grp", "rep"))),
        check_vma=False,
    )
```

time: 309 us -> 275 us (0.89)
  waiting for transfers between devices: 82.5 us -> 37.7 us
  blocking collectives: 0 us -> 38.1 us
  local copies, waits for them, and re-layouts: 80.9 us -> 60.7 us
  other arithmetic: 55.6 us -> 50.5 us
    all_to_all x1, waiting for transfers between devices: 29.4 us -> 0.01 us  [per_device(): lax.all_to_all(outgoing, ('grp', 'rep'), split_axis=0, concat_axis=0, til...]
    reduce_scatter x1 -> x0, waiting for transfers between devices: 24.1 us -> none  [per_device(): lax.psum_scatter(jnp.einsum('bc,bo->co', slope_pos, queries, preferred_el...]
    gather x4, local copies, waits for them, and re-layouts: 42 us -> 18.7 us  [the longest x1 12.1 us: per_device(): outgoing = item_vec[row_ids] * live_mask[..., None].astype(jnp.bfloat16)]
    unnamed x0 -> x1, blocking collectives: none -> 21.7 us
    all_gather x1, waiting for transfers between devices: 0.01 us -> 19 us  [per_device(): group_queries = lax.all_gather(queries, 'grp', axis=0, tiled=True)]
    all_gather x0 -> x1, blocking collectives: none -> 16.4 us  [per_device(): group_rate = lax.all_gather(rate, 'grp', axis=0, tiled=True)]
    all_to_all x1, waiting for transfers between devices: 28.9 us -> 18.7 us  [per_device(): lax.all_to_all(slot_grads.astype(jnp.bfloat16).reshape(peer_count, cap_sl...]
  transfers between devices with their start and end apart: 4 -> 3, of which waited for: 3 -> 2; matrix products, arithmetic and copies ran while one was open for 16% -> 17% of each run, Pallas kernels for 0% -> 0%
where the time goes in v1:
time: 275 us; the launch traced here: 274 us
  local copies, waits for them, and re-layouts  60.7 us (22%)
  matrix products  52.8 us (19%)
  other arithmetic  50.5 us (18%)
  blocking collectives  38.1 us (14%)
  waiting for transfers between devices  37.7 us (14%)
  starting transfers between devices  19.3 us (7%)
  between operations  15.1 us (5%)
    gather x1, local copies, waits for them, and re-layouts, per_device(): user_table[user_ids].astype(jnp.float32)  33.9 us
    scatter-add x1, other arithmetic, per_device(): row_grads.at[row_ids.reshape(-1)].add(values.reshape(-1, unit.shape[1]))  24 us
    unnamed x1, blocking collectives  21.7 us
    all_gather x1, waiting for transfers between devices, per_device(): group_queries = lax.all_gather(queries, 'grp', axis=0, tiled=True)  19 us
    all_to_all x1, waiting for transfers between devices, per_device(): lax.all_to_all(slot_grads.astype(jnp.bfloat16).reshape(peer_count, cap_sl...  18.7 us
    all_gather x1, blocking collectives, per_device(): group_rate = lax.all_gather(rate, 'grp', axis=0, tiled=True)  16.4 us
    dot_general x1, matrix products, per_device(): jnp.einsum('bo,co->bc', group_queries, positive, preferred_element_type=j...  16.3 us
    dot_general x1, matrix products, per_device(): jnp.einsum('bc,bo->co', pos_exp.astype(jnp.bfloat16), (group_queries.asty...  15.1 us
  transfers between devices with their start and end apart: 3, of which 2 were waited for; matrix products, arithmetic and copies ran while one was open for 17% of the time, Pallas kernels for 0%

profile of v1, /device:TPU:1, one launch (start us, length us, event | category | flops | bytes accessed | tf_op | source)
XLA Modules:
  0.0 274.3 jit_solution(2973136343170407768)
XLA Ops:
  8.8 2.2 fusion.40
  11.0 3.2 %multiply_reduce_fusion.1 = (f32[4096]{0:T(1024)S(1)}, f32[4096,128]{0,1:T(8,128)S(1)}) fusion(bf16[512,128]{1,0:T(8,128)(2,1)S(1)} %copy-done.14, f32[4096,512]{1,0:T(8,128)S(1)} %fusion.40), kind=kOutput, calls=%fused_computation.27 | convolution fusion | flops 548401152 | bytes 10633216 | tf_op jit(solution)/shard_map/dot_general | solution.py:13
  16.7 12.1 %gather_fusion.1 = bf16[4096,128]{1,0:T(8,128)(2,1)S(1)} fusion(bf16[4096,128]{1,0:T(8,128)(2,1)S(1)} %copy.29, s32[4096]{0:T(1024)S(1)} %broadcast_clamp_fusion.1), kind=kCustom, calls=%fused_computation.1 | custom fusion | bytes 2113536 | tf_op jit(solution)/shard_map/gather | solution.py:43
  30.4 11.5 %all-to-all-start = ((bf16[128,32,128]{2,1,0:T(8,128)(2,1)}), bf16[128,32,128]{2,1,0:T(8,128)(2,1)S(1)}, u32[]{:S(2)}, u32[]{:S(2)}) async-start(bf16[128,32,128]{2,1,0:T(8,128)(2,1)} %broadcast_multiply_fusion), calls=%async_computation | async-start | bytes 2097152 | tf_op jit(solution)/shard_map/all_to_all | solution.py:44
  42.6 33.9 %gather_fusion = bf16[8192,256]{1,0:T(8,128)(2,1)} fusion(bf16[8192,256]{1,0:T(8,128)(2,1)} %param.17, s32[8192]{0:T(1024)S(1)} %broadcast_clamp_fusion), kind=kCustom, calls=%fused_computation | custom fusion | bytes 8421376 | tf_op jit(solution)/shard_map/gather | solution.py:37
  76.5 5.1 %bitcast_reduce_fusion = bf16[1024,256]{1,0:T(8,128)(2,1)S(1)} fusion(bf16[8192,256]{1,0:T(8,128)(2,1)} %gather_fusion), kind=kLoop, calls=%fused_computation.15 | loop fusion | flops 1835008 | bytes 4718592 | tf_op jit(solution)/shard_map/reduce_sum | solution.py:37
  82.6 3.2 %gather_fusion.2 = bf16[1024,128]{1,0:T(8,128)(2,1)S(1)} fusion(bf16[4096,128]{1,0:T(8,128)(2,1)S(1)} %bitcast.28, s32[1024]{0:T(1024)S(1)} %get-tuple-element.8), kind=kCustom, calls=%fused_computation.2 | custom fusion | bytes 528384 | tf_op jit(solution)/shard_map/gather | solution.py:46
  88.1 3.2 %gather_fusion.3 = bf16[1024,128]{1,0:T(8,128)(2,1)S(1)} fusion(bf16[4096,128]{1,0:T(8,128)(2,1)S(1)} %bitcast.29, s32[1024]{0:T(1024)S(1)} %broadcast_clamp_fusion.2), kind=kCustom, calls=%fused_computation.3 | custom fusion | bytes 528384 | tf_op jit(solution)/shard_map/gather | solution.py:47
  91.3 3.7 %fusion.6 = (f32[1024]{0:T(1024)S(1)}, f32[1024,1024]{0,1:T(8,128)}) fusion(bf16[1024,128]{1,0:T(8,128)(2,1)S(1)} %gather_fusion.3, bf16[1024,128]{0,1:T(8,128)(2,1)} %get-tuple-element.5), kind=kOutput, calls=%fused_computation.20 | convolution fusion | flops 270531584 | bytes 4722688 | tf_op jit(solution)/shard_map/bo,co->bc/dot_general | solution.py:51
  94.9 19.0 %all-gather.2.cloned.1.call-done = bf16[8192,128]{0,1:T(8,128)(2,1)} async-done(((bf16[1024,128]{0,1:T(8,128)(2,1)}), bf16[8192,128]{0,1:T(8,128)(2,1)}) %all-gather.2.cloned.1.call-update) | async-done | bytes 2097168 | tf_op jit(solution)/shard_map/all_gather | solution.py:39
  113.9 16.3 %fusion = (f32[8192]{0:T(1024)S(1)}, f32[8192,1024]{0,1:T(8,128)}) fusion(s32[1024]{0:T(1024)S(1)} %iota_add_fusion, bf16[1024,128]{1,0:T(8,128)(2,1)S(1)} %gather_fusion.2, bf16[8192,128]{0,1:T(8,128)(2,1)} %all-gather.2.cloned.1.call-done), kind=kOutput, calls=%fused_computation.9 | convolution fusion | flops 2181029888 | bytes 35950592 | tf_op jit(solution)/shard_map/bo,co->bc/dot_general | solution.py:60
  130.2 21.7 %all-reduce = f32[8192]{0:T(1024)S(1)} all-reduce(f32[8192]{0:T(1024)S(1)} %get-tuple-element.18), channel_id=2, replica_groups=mesh['grp'=8,'rep'=16] {'grp'}, use_global_device_ids=true, to_apply=%region_4.5.clone | all-reduce | flops 8192 | bytes 65536
  152.5 16.4 %all_gather.7 = f32[8192]{0:T(1024)S(1)} all-gather(f32[1024]{0:T(1024)S(1)} %get-tuple-element.7), channel_id=1, replica_groups=mesh['grp'=8,'rep'=16] {'grp'}, dimensions={0}, use_global_device_ids=true | all-gather | bytes 36864 | tf_op jit(solution)/shard_map/all_gather | solution.py:72
  168.9 2.9 %fusion.7 = f32[1024,128]{1,0:T(8,128)S(1)} fusion(f32[1024,1024]{0,1:T(8,128)} %get-tuple-element.17, bf16[1024,128]{0,1:T(8,128)(2,1)S(1)} %copy-done.5, f32[1024]{0:T(1024)S(1)} %get-tuple-element.7), kind=kOutput, calls=%fused_computation.21 | convolution fusion | flops 270925824 | bytes 4984832 | tf_op jit(solution)/shard_map/bc,bo->co/dot_general | solution.py:74
  171.8 15.1 %fusion.13 = f32[1024,128]{0,1:T(8,128)S(1)} fusion(bf16[8192,128]{0,1:T(8,128)(2,1)} %all-gather.2.cloned.1.call-done, f32[8192]{0:T(1024)S(1)} %all_gather.7, f32[8192,1024]{0,1:T(8,128)} %get-tuple-element.19, s32[1024]{0:T(1024)S(1)} %iota_add_fusion, bf16[1024,128]{0,1:T(8,128)(2,1)S(1)} %copy-done.5, f32[1024]{0:T(1024)S(1)} %get-tuple-element.6), kind=kOutput, calls=%fused_computation.31 | convolution fusion | flops 2184577024 | bytes 36478976 | tf_op jit(solution)/shard_map/bc,bo->co/dot_general | solution.py:80
  187.1 6.5 %scatter_custom_fusion = f32[4096,128]{1,0:T(8,128)S(1)} fusion(s32[1024]{0:T(1024)S(1)} %get-tuple-element.9, f32[1024,128]{1,0:T(8,128)S(1)} %copy.32, f32[]{:T(128)} %constant.11.clone.1), kind=kCustom, calls=%fused_computation.38 | custom fusion | flops 131072 | bytes 2097156 | tf_op jit(solution)/shard_map/scatter-add | solution.py:88
  193.7 6.8 %scatter_fusion = f32[4096,128]{1,0:T(8,128)S(1)} fusion(f32[4096,128]{1,0:T(8,128)S(1)} %scatter_custom_fusion, s32[1024]{0:T(1024)S(1)} %bitcast.34, f32[1024,128]{1,0:T(8,128)S(1)} %fusion.7), kind=kCustom, calls=%fused_computation.5 | custom fusion | flops 131072 | bytes 1576960 | tf_op jit(solution)/shard_map/scatter-add | solution.py:88
  201.5 7.6 %all-to-all-start.1 = ((bf16[128,32,128]{2,1,0:T(8,128)(2,1)}), bf16[128,32,128]{2,1,0:T(8,128)(2,1)S(1)}, u32[]{:S(2)}, u32[]{:S(2)}) async-start(bf16[128,32,128]{2,1,0:T(8,128)(2,1)} %bitcast.30), calls=%async_computation.1 | async-start | bytes 2097152 | tf_op jit(solution)/shard_map/all_to_all | solution.py:89
  209.4 18.7 %all-to-all-done.1 = bf16[128,32,128]{2,1,0:T(8,128)(2,1)S(1)} async-done(((bf16[128,32,128]{2,1,0:T(8,128)(2,1)}), bf16[128,32,128]{2,1,0:T(8,128)(2,1)S(1)}, u32[]{:S(2)}, u32[]{:S(2)}) %all-to-all-start.1) | async-done | bytes 1048608 | tf_op jit(solution)/shard_map/all_to_all | solution.py:89
  228.0 1.9 convert_multiply_fusion
  230.0 24.0 %scatter_custom_fusion.2 = f32[4096,128]{1,0:T(8,128)} fusion(s32[4096]{0:T(1024)S(1)} %bitcast.35, f32[4096,128]{1,0:T(8,128)} %bitcast.32, f32[]{:T(128)} %constant.11.clone.1), kind=kCustom, calls=%fused_computation.36 | custom fusion | flops 524288 | bytes 2097664 | tf_op jit(solution)/shard_map/scatter-add | solution.py:98
  254.0 3.0 %copy.34 = f32[4096,128]{0,1:T(8,128)} copy(f32[4096,128]{1,0:T(8,128)} %scatter_custom_fusion.2) | data formatting | bytes 4194304 | tf_op jit(solution)/shard_map/scatter-add | solution.py:98
  257.0 1.9 multiply_reduce_fusion
  258.8 8.6 %fusion.11 = f32[4096,256]{1,0:T(8,128)} fusion(bf16[256,512]{1,0:T(8,128)(2,1)S(1)} %copy-done.6, f32[4096,512]{1,0:T(8,128)} %copy-done.2, bf16[512,128]{1,0:T(8,128)(2,1)S(1)} %copy-done.14, f32[4096,128]{0,1:T(8,128)} %copy.34, f32[4096]{0:T(1024)S(1)} %multiply_reduce_fusion, f32[4096]{0:T(1024)S(1)} %add_sqrt_fusion, f32[4096,128]{0,1:T(8,128)} %copy-done.3), kind=kOutput, calls=%fused_computation.29 | convolution fusion | flops 1632108544 | bytes 17203200 | tf_op jit(solution)/shard_map/sh,eh->se/dot_general | solution.py:105
  (64 shorter events, 10.8 us)
Async XLA Ops:
  7.2 1.6 copy-start
  7.2 3.8 %copy-start.14 = (bf16[512,128]{1,0:T(8,128)(2,1)S(1)}, bf16[512,128]{1,0:T(8,128)(2,1)}, u32[]{:S(2)}) copy-start(bf16[512,128]{1,0:T(8,128)(2,1)} %param.19) | copy-start | bytes 393220
  11.0 3.2 %copy-start.2 = (f32[4096,512]{1,0:T(8,128)}, f32[4096,512]{1,0:T(8,128)S(1)}, u32[]{:S(2)}) copy-start(f32[4096,512]{1,0:T(8,128)S(1)} %fusion.40) | copy-start | bytes 25165828
  14.2 1.4 copy-start.3
  14.2 2.2 copy-start.7
  14.2 2.4 copy-start.11
  28.8 13.3 %copy-start.8 = (s32[1024,8]{0,1:T(8,128)S(1)}, s32[1024,8]{0,1:T(8,128)}, u32[]{:S(2)}) copy-start(s32[1024,8]{0,1:T(8,128)} %param.16) | copy-start | bytes 98308
  30.4 52.2 %all-to-all-start = ((bf16[128,32,128]{2,1,0:T(8,128)(2,1)}), bf16[128,32,128]{2,1,0:T(8,128)(2,1)S(1)}, u32[]{:S(2)}, u32[]{:S(2)}) async-start(bf16[128,32,128]{2,1,0:T(8,128)(2,1)} %broadcast_multiply_fusion), calls=%async_computation | async-start | bytes 2097152 | tf_op jit(solution)/shard_map/all_to_all | solution.py:44
  41.9 72.0 %all-gather.2.cloned.1.call-start = ((), (), s32[]{:S(2)}) async-start(), calls=%async_computation.2 | async-start | bytes 2359296 | tf_op jit(solution)/shard_map/all_gather | solution.py:39
  76.5 5.1 %copy-start.12 = (bf16[256,512]{1,0:T(8,128)(2,1)S(1)}, bf16[256,512]{1,0:T(8,128)(2,1)}, u32[]{:S(2)}) copy-start(bf16[256,512]{1,0:T(8,128)(2,1)} %param.20) | copy-start | bytes 786436
  76.5 5.1 %copy-start.13 = (bf16[512,128]{1,0:T(8,128)(2,1)S(1)}, bf16[512,128]{1,0:T(8,128)(2,1)}, u32[]{:S(2)}) copy-start(bf16[512,128]{1,0:T(8,128)(2,1)} %param.21) | copy-start | bytes 393220
  81.6 1.0 copy-start.9
  82.5 4.3 %copy-start.15 = (u32[128]{0:T(128)S(1)}, u32[128]{0:T(128)}, u32[]{:S(2)}) copy-start(u32[128]{0:T(128)} %constant.42) | copy-start | bytes 1540
  82.5 5.5 %copy-start.10 = (s32[1,1024]{1,0:T(1,128)S(1)}, s32[1,1024]{1,0:T(1,128)}, u32[]{:S(2)}) copy-start(s32[1,1024]{1,0:T(1,128)} %param.15) | copy-start | bytes 12292
  94.9 74.0 %copy-start.5 = (bf16[1024,128]{0,1:T(8,128)(2,1)S(1)}, bf16[1024,128]{0,1:T(8,128)(2,1)}, u32[]{:S(2)}) copy-start(bf16[1024,128]{0,1:T(8,128)(2,1)} %get-tuple-element.5) | copy-start | bytes 786436
  201.5 26.5 %all-to-all-start.1 = ((bf16[128,32,128]{2,1,0:T(8,128)(2,1)}), bf16[128,32,128]{2,1,0:T(8,128)(2,1)S(1)}, u32[]{:S(2)}, u32[]{:S(2)}) async-start(bf16[128,32,128]{2,1,0:T(8,128)(2,1)} %bitcast.30), calls=%async_computation.1 | async-start | bytes 2097152 | tf_op jit(solution)/shard_map/all_to_all | solution.py:89
  228.0 28.9 %copy-start.4 = (f32[4096,128]{0,1:T(8,128)S(1)}, f32[4096,128]{0,1:T(8,128)}, u32[]{:S(2)}) copy-start(f32[4096,128]{0,1:T(8,128)} %copy-done.3) | copy-start | bytes 6291460
  254.0 4.8 %copy-start.6 = (bf16[256,512]{1,0:T(8,128)(2,1)S(1)}, bf16[256,512]{1,0:T(8,128)(2,1)}, u32[]{:S(2)}) copy-start(bf16[256,512]{1,0:T(8,128)(2,1)} %param.18) | copy-start | bytes 786436
  258.8 8.6 %copy-start.1 = (bf16[4096,256]{1,0:T(8,128)(2,1)S(1)}, bf16[4096,256]{1,0:T(8,128)(2,1)}, u32[]{:S(2)}) copy-start(bf16[4096,256]{1,0:T(8,128)(2,1)} %param.11) | copy-start | bytes 6291460
Sparse Core Ops, SparseCore 0:
  86.9 27.0 all-gather.1

commit v2 on v0

v2 whole, which is shorter than its diff:
```python
import functools
import math

import jax
import jax.numpy as jnp
from jax import lax
from jax.experimental import pallas as pl
from jax.experimental.pallas import tpu as pltpu
from jax.sharding import PartitionSpec as P

LOGIT_SCALE = 20.0
NORM_EPS = 1e-06
LOG2E = math.log2(math.e)
MESH = pl.DeviceIdType.MESH
VMEM = pl.BlockSpec(memory_space=pltpu.VMEM)
SMEM = pl.BlockSpec(memory_space=pltpu.SMEM)
F32, BF16 = jnp.float32, jnp.bfloat16


def mm(a, b):
    return jnp.dot(a, b, preferred_element_type=F32)


def mm_t(a, b):
    return lax.dot_general(a, b, (((1,), (1,)), ((), ())), preferred_element_type=F32)


def tower(x, w1, w2):
    pre = mm(x, w1)
    sig = 0.5 + 0.5 * jnp.tanh(0.5 * pre)
    out = mm((pre * sig).astype(BF16), w2)
    inv = lax.rsqrt(jnp.sum(out * out, axis=-1, keepdims=True) + NORM_EPS)
    return pre, sig, inv, out * inv


def params(**kw):
    return pltpu.CompilerParams(vmem_limit_bytes=56 * 2**20, **kw)


def item_kernel(rows, table, w1, w2, out, unit, picked):
    n = table.shape[0]
    unit[pl.ds(n, 8), :] = jnp.zeros((8, unit.shape[1]), F32)

    def forward(i, c):
        at = pl.ds(i * 256, 256)
        unit[at, :] = tower(table[at, :], w1[...], w2[...])[3]
        return c

    lax.fori_loop(0, n // 256, forward, 0)

    def gather(t, c):
        for j in range(32):
            picked[pl.ds(t * 32 + j, 1), :] = unit[pl.ds(rows[t * 32 + j], 1), :]
        at = pl.ds(t * 32, 32)
        out[at, :] = picked[at, :].astype(BF16)
        return c

    lax.fori_loop(0, out.shape[0] // 32, gather, 0)


def user_kernel(ids, table, w1, w2, out, low, high, plow, phigh):
    half = table.shape[1] // 2
    feat = ids.shape[0] // out.shape[0]

    def widen(i, c):
        at = pl.ds(i * 128, 128)
        low[at, :] = table[at, :half].astype(F32)
        high[at, :] = table[at, half:].astype(F32)
        return c

    lax.fori_loop(0, table.shape[0] // 128, widen, 0)

    def pool(i, c):
        for k in range(8):
            b = i * 8 + k
            at = [pl.ds(ids[b * feat + f], 1) for f in range(feat)]
            lo = [low[a, :] for a in at]
            hi = [high[a, :] for a in at]
            while len(lo) > 1:
                lo = [x + y for x, y in zip(lo[::2], lo[1::2])]
                hi = [x + y for x, y in zip(hi[::2], hi[1::2])]
            plow[pl.ds(b, 1), :] = lo[0]
            phigh[pl.ds(b, 1), :] = hi[0]
        return c

    lax.fori_loop(0, out.shape[0] // 8, pool, 0)

    def forward(i, c):
        at = pl.ds(i * 256, 256)
        x = jnp.concatenate([plow[at, :], phigh[at, :]], axis=1).astype(BF16)
        out[at, :] = tower(x, w1[...], w2[...])[3].astype(BF16)
        return c

    lax.fori_loop(0, out.shape[0] // 256, forward, 0)


def score_kernel(
    pos_slot, neg_slot, queries, slots, pos_grad, neg_grad, loss,
    wide, picked, cols, group, pexp, nexp, sums_out, sums_in, rates,
    q_send, q_recv, f_send, f_recv, s_send, s_recv, r_send, r_recv,
):
    users = queries.shape[0]
    peers = group.shape[0]
    chips = peers // 2
    me = lax.axis_index("grp")
    chip, core = me // 2, lax.rem(me, 2)
    sib = chip * 2 + 1 - core

    def there(k):
        return lax.rem(chip + k, chips) * 2 + core

    barrier = pltpu.get_barrier_semaphore()
    for k in range(1, peers):
        pl.semaphore_signal(
            barrier, inc=1, device_id={"grp": lax.rem(me + k, peers)}, device_id_type=MESH
        )
    pl.semaphore_wait(barrier, peers - 1)

    def push(src, dst, ss, rs, to):
        return pltpu.make_async_remote_copy(
            src_ref=src, dst_ref=dst, send_sem=ss, recv_sem=rs,
            device_id={"grp": to}, device_id_type=MESH,
        )

    group[0] = queries[...]
    q_copies = []
    for k in range(1, chips):
        q_copies.append(
            push(queries, group.at[k], q_send.at[k], q_recv.at[k], there(chips - k))
        )
        q_copies[-1].start()
    f_copies = [push(queries, group.at[chips], f_send.at[0], f_recv.at[0], sib)]
    f_copies[0].start()
    for k in range(1, chips):
        f_copies.append(
            push(group.at[k], group.at[chips + k], f_send.at[k], f_recv.at[k], sib)
        )

    def widen(i, c):
        at = pl.ds(i * 256, 256)
        wide[at, :] = slots[at, :].astype(F32)
        return c

    lax.fori_loop(0, slots.shape[0] // 256, widen, 0)

    def gather(i, c):
        for j in range(16):
            picked[pl.ds(i * 16 + j, 1), :] = wide[pl.ds(neg_slot[i * 16 + j], 1), :]
        for j in range(16):
            picked[pl.ds(users + i * 16 + j, 1), :] = wide[pl.ds(pos_slot[i * 16 + j], 1), :]
        return c

    lax.fori_loop(0, users // 16, gather, 0)

    def narrow(i, c):
        at = pl.ds(i * 256, 256)
        cols[at, :] = picked[at, :].astype(BF16)
        return c

    lax.fori_loop(0, cols.shape[0] // 256, narrow, 0)

    step = 128

    def block(q, first, store, diag):
        def part(i, carry):
            total, own = carry
            s = mm_t(cols[pl.ds(first + i * step, step), :], q)
            e = jnp.exp2(s * (LOGIT_SCALE * LOG2E))
            if diag:
                hit = (
                    lax.broadcasted_iota(jnp.int32, s.shape, 0) + i * step
                    == lax.broadcasted_iota(jnp.int32, s.shape, 1)
                )
                e = jnp.where(hit, 0.0, e)
                own = own + jnp.sum(jnp.where(hit, s, 0.0), axis=0, keepdims=True)
            store(i, e.astype(BF16))
            return total + jnp.sum(e, axis=0, keepdims=True), own

        zero = jnp.zeros((1, users), F32)
        return lax.fori_loop(0, users // step, part, (zero, zero))

    def store_neg(i, e):
        nexp[pl.ds(i * step, step), :] = e

    def store_pos(k):
        def store(i, e):
            pexp[k, pl.ds(i * step, step), :] = e

        return store

    neg_sum, _ = block(group[0], 0, store_neg, False)
    own_sum, own_score = block(group[0], users, store_pos(0), True)
    own_score = own_score * LOGIT_SCALE

    s_copies = []
    order = [chips]
    for k in range(1, chips):
        order += [k, chips + k]
    for k in order:
        if k >= chips:
            f_copies[k - chips].wait_recv()
        else:
            q_copies[k - 1].wait_recv()
            f_copies[k].start()
        total, _ = block(group[k], users, store_pos(k), False)
        sums_out[k] = total
        kk = k % chips
        back = (chips - kk) % chips + (chips if k >= chips else 0)
        to = lax.rem(chip + kk, chips) * 2 + (1 - core if k >= chips else core)
        s_copies.append(push(sums_out.at[k], sums_in.at[back], s_send.at[k], s_recv.at[back], to))
        s_copies[-1].start()
    for c in s_copies:
        c.wait_recv()

    other = neg_sum + own_sum
    for k in range(1, peers):
        other = other + sums_in[k]
    total = other + jnp.exp2(own_score * LOG2E)
    loss[...] = jnp.log(total) - own_score
    rate = LOGIT_SCALE / total
    rates[0] = rate
    r_copies = []
    for k in order:
        kk = k % chips
        back = (chips - kk) % chips + (chips if k >= chips else 0)
        to = lax.rem(chip + kk, chips) * 2 + (1 - core if k >= chips else core)
        r_copies.append(push(rates.at[0], rates.at[back], r_send.at[k], r_recv.at[back], to))
        r_copies[-1].start()

    def upright(row):
        return jnp.transpose(jnp.broadcast_to(row, (128, users)))

    q_own = group[0].astype(F32)
    scaled = (q_own * upright(rate)).astype(BF16)

    def own_part(i, c):
        at = pl.ds(i * 256, 256)
        neg_grad[at, :] = mm(nexp[at, :], scaled)
        pos_grad[at, :] = mm(pexp[0, at, :], scaled)
        return c

    lax.fori_loop(0, users // 256, own_part, 0)
    pos_grad[...] = pos_grad[...] - q_own * upright(rate * other)

    for c in r_copies:
        c.wait_recv()

    for k in order:
        scaled_k = (group[k].astype(F32) * upright(rates[k])).astype(BF16)

        def far_part(i, c):
            at = pl.ds(i * 256, 256)
            pos_grad[at, :] = pos_grad[at, :] + mm(pexp[k, at, :], scaled_k)
            return c

        lax.fori_loop(0, users // 256, far_part, 0)

    for c in q_copies + f_copies + s_copies + r_copies:
        c.wait_send()


def slot_kernel(pos_slot, neg_slot, pos_grad, neg_grad, out, *acc):
    n = out.shape[0]
    half = pos_slot.shape[0] // 2

    def clear(i, c):
        for a in acc:
            a[pl.ds(i * 128, 128), :] = jnp.zeros((128, a.shape[1]), F32)
        return c

    lax.fori_loop(0, n // 128, clear, 0)
    chains = [
        (pos_slot, pos_grad, 0), (neg_slot, neg_grad, 0),
        (pos_slot, pos_grad, half), (neg_slot, neg_grad, half),
    ]

    def scatter(i, c):
        for j in range(8):
            at = [pl.ds(slot[first + i * 8 + j], 1) for slot, _, first in chains]
            new = [
                a[r, :] + grad[pl.ds(first + i * 8 + j, 1), :]
                for a, r, (_, grad, first) in zip(acc, at, chains)
            ]
            for a, r, v in zip(acc, at, new):
                a[r, :] = v
        return c

    lax.fori_loop(0, half // 8, scatter, 0)

    def merge(i, c):
        at = pl.ds(i * 128, 128)
        out[at, :] = (acc[0][at, :] + acc[1][at, :] + (acc[2][at, :] + acc[3][at, :])).astype(BF16)
        return c

    lax.fori_loop(0, n // 128, merge, 0)


def back_kernel(rows, back, table, w1, w2, out, acc, wide):
    n = table.shape[0]

    def prepare(i, c):
        at = pl.ds(i * 128, 128)
        acc[at, :] = jnp.zeros((128, acc.shape[1]), F32)
        wide[at, :] = back[at, :].astype(F32)
        return c

    lax.fori_loop(0, n // 128, prepare, 0)

    def scatter(t, c):
        at = [pl.ds(rows[t * 32 + j], 1) for j in range(32)]
        new = [acc[r, :] + wide[pl.ds(t * 32 + j, 1), :] for j, r in enumerate(at)]
        for r, v in zip(at, new):
            acc[r, :] = v
        return c

    lax.fori_loop(0, wide.shape[0] // 32, scatter, 0)

    def backward(i, c):
        at = pl.ds(i * 256, 256)
        pre, sig, inv, unit = tower(table[at, :], w1[...], w2[...])
        g = acc[at, :]
        radial = jnp.sum(unit * g, axis=-1, keepdims=True)
        d_out = ((g - unit * radial) * inv).astype(BF16)
        d_hid = mm_t(d_out, w2[...])
        d_pre = (d_hid * sig * (1.0 + pre * (1.0 - sig))).astype(BF16)
        out[at, :] = mm_t(d_pre, w1[...])
        return c

    lax.fori_loop(0, n // 256, backward, 0)


def per_device(
    item_table, send_rows, send_count, pos_slot, neg_slot, user_ids,
    user_table, item_w1, item_w2, user_w1, user_w2,
):
    peers, cap = send_rows.shape[1:]
    slots = peers * cap
    n, users, negs = item_table.shape[0], pos_slot.shape[0], neg_slot.shape[1]
    vocab, outw = user_table.shape[0], item_w2.shape[1]
    grp = lax.axis_size("grp")
    live = jnp.arange(cap, dtype=jnp.int32)[None, :] < send_count[0][:, None]
    rows = jnp.where(live, send_rows[0], n).reshape(-1)
    neg = neg_slot.reshape(-1)

    outgoing = pl.pallas_call(
        item_kernel,
        out_shape=jax.ShapeDtypeStruct((slots, outw), BF16),
        in_specs=[SMEM] + [VMEM] * 3,
        out_specs=VMEM,
        scratch_shapes=[pltpu.VMEM((n + 8, outw), F32), pltpu.VMEM((slots, outw), F32)],
        compiler_params=params(),
        cost_estimate=pl.CostEstimate(flops=2 * n * 512 * 384, bytes_accessed=2**22, transcendentals=n * 512),
        name="items",
    )(rows, item_table, item_w1, item_w2)
    arrived = lax.all_to_all(
        outgoing.reshape(peers, cap, outw), ("grp", "rep"), split_axis=0, concat_axis=0, tiled=True
    ).reshape(slots, outw)

    queries = pl.pallas_call(
        user_kernel,
        out_shape=jax.ShapeDtypeStruct((users, outw), BF16),
        in_specs=[SMEM] + [VMEM] * 3,
        out_specs=VMEM,
        scratch_shapes=[pltpu.VMEM((vocab, 128), F32)] * 2 + [pltpu.VMEM((users, 128), F32)] * 2,
        compiler_params=params(),
        cost_estimate=pl.CostEstimate(flops=2**33, bytes_accessed=2**24, transcendentals=users * 512),
        name="users",
    )(user_ids.reshape(-1), user_table, user_w1, user_w2)

    dma = pltpu.SemaphoreType.DMA
    pos_grad, neg_grad, loss = pl.pallas_call(
        score_kernel,
        out_shape=[
            jax.ShapeDtypeStruct((users, outw), F32),
            jax.ShapeDtypeStruct((negs, outw), F32),
            jax.ShapeDtypeStruct((1, users), F32),
        ],
        in_specs=[SMEM, SMEM, VMEM, VMEM],
        out_specs=[VMEM] * 3,
        scratch_shapes=[
            pltpu.VMEM((slots, outw), F32),
            pltpu.VMEM((users + negs, outw), F32),
            pltpu.VMEM((users + negs, outw), BF16),
            pltpu.VMEM((grp, users, outw), BF16),
            pltpu.VMEM((grp, users, users), BF16),
            pltpu.VMEM((negs, users), BF16),
            pltpu.VMEM((grp, 1, users), F32),
            pltpu.VMEM((grp, 1, users), F32),
            pltpu.VMEM((grp, 1, users), F32),
            dma((grp // 2,)), dma((grp // 2,)), dma((grp // 2,)), dma((grp // 2,)),
            dma((grp,)), dma((grp,)), dma((grp,)), dma((grp,)),
        ],
        compiler_params=params(collective_id=0, has_side_effects=True),
        cost_estimate=pl.CostEstimate(flops=2**32, bytes_accessed=2**22, transcendentals=2**23),
        name="scores",
    )(pos_slot, neg, queries, arrived)

    slot_grads = pl.pallas_call(
        slot_kernel,
        out_shape=jax.ShapeDtypeStruct((slots, outw), BF16),
        in_specs=[SMEM, SMEM, VMEM, VMEM],
        out_specs=VMEM,
        scratch_shapes=[pltpu.VMEM((slots, outw), F32)] * 4,
        compiler_params=params(),
        name="slot_sums",
    )(pos_slot, neg, pos_grad, neg_grad)
    returned = lax.all_to_all(
        slot_grads.reshape(peers, cap, outw), ("grp", "rep"), split_axis=0, concat_axis=0, tiled=True
    ).reshape(slots, outw)

    table_grad = pl.pallas_call(
        back_kernel,
        out_shape=jax.ShapeDtypeStruct(item_table.shape, F32),
        in_specs=[SMEM] + [VMEM] * 4,
        out_specs=VMEM,
        scratch_shapes=[pltpu.VMEM((n + 8, outw), F32), pltpu.VMEM((slots, outw), F32)],
        compiler_params=params(),
        name="row_grads",
    )(rows, returned, item_table, item_w1, item_w2)
    return table_grad, loss.reshape(-1)


def solution(mesh):
    return jax.shard_map(
        per_device,
        mesh=mesh,
        in_specs=(
            P(("grp", "rep"), None),
            P(("grp", "rep"), None, None),
            P(("grp", "rep"), None),
            P(("grp", "rep")),
            P(("grp", "rep"), None),
            P(("grp", "rep"), None),
            P(), P(), P(), P(), P(),
        ),
        out_specs=(P(("grp", "rep"), None), P(("grp", "rep"))),
        check_vma=False,
    )
```

time: 309 us -> 151 us (0.49)
  Pallas kernels: 0 us -> 105 us
  local copies, waits for them, and re-layouts: 80.9 us -> 4.56 us
  waiting for transfers between devices: 82.5 us -> 21.2 us
  other arithmetic: 55.6 us -> 1.35 us
  matrix products: 52.1 us -> 0 us
  between operations: 14.4 us -> 0.71 us
  starting transfers between devices: 22.1 us -> 17.8 us
    pallas_call x0 -> x5, Pallas kernels: none -> 105 us  [the longest x1 42 us: per_device(): pl.pallas_call(score_kernel, out_shape=[jax.ShapeDtypeStruct((users, outw...]
    gather x5 -> x0, local copies, waits for them, and re-layouts: 76 us -> none  [the longest x1 34.1 us: per_device(): user_table[user_ids].astype(jnp.float32)]
    dot_general x8 -> x0, matrix products: 52.1 us -> none  [the longest x1 18.1 us: per_device(): jnp.einsum('bc,bo->co', slope_pos, queries, preferred_element_type=jnp.fl...]
    scatter-add x3 -> x0, other arithmetic: 38.8 us -> none  [the longest x1 25.1 us: per_device(): table_grad.at[row_ids.reshape(-1)].add(values.reshape(-1, emb_width))]
    all_to_all x2, waiting for transfers between devices: 58.3 us -> 21.2 us  [the longest x1 18.9 us: per_device(): lax.all_to_all(slot_grads.reshape(peers, cap, outw), ('grp', 'rep'), spli...]
    reduce_scatter x1 -> x0, waiting for transfers between devices: 24.1 us -> none  [per_device(): lax.psum_scatter(jnp.einsum('bc,bo->co', slope_pos, queries, preferred_el...]
    reduce_sum x2 -> x0, other arithmetic: 7.69 us -> none  [the longest x1 5.03 us: per_device(): jnp.sum(user_table[user_ids].astype(jnp.float32), axis=1)]
    mul x2 -> x0, other arithmetic: 6.58 us -> none  [the longest x1 3.65 us: per_device(): returned.astype(jnp.float32) * live_mask[..., None].astype(jnp.float32)]
  transfers between devices with their start and end apart: 4 -> 2, of which waited for: 3 -> 2; matrix products, arithmetic and copies ran while one was open for 16% -> 1% of each run, Pallas kernels for 0% -> 10%
where the time goes in v2:
time: 151 us
  Pallas kernels  105 us (70%)
  waiting for transfers between devices  21.2 us (14%)
  starting transfers between devices  17.8 us (12%)
  local copies, waits for them, and re-layouts  4.56 us (3%)
    pallas_call x1, Pallas kernels, per_device(): pl.pallas_call(score_kernel, out_shape=[jax.ShapeDtypeStruct((users, outw...  42 us
    pallas_call x1, Pallas kernels, per_device(): pl.pallas_call(back_kernel, out_shape=jax.ShapeDtypeStruct(item_table.sha...  26.4 us
    all_to_all x1, waiting for transfers between devices, per_device(): lax.all_to_all(slot_grads.reshape(peers, cap, outw), ('grp', 'rep'), spli...  18.9 us
    pallas_call x1, Pallas kernels, per_device(): pl.pallas_call(user_kernel, out_shape=jax.ShapeDtypeStruct((users, outw),...  15.5 us
    pallas_call x1, Pallas kernels, per_device(): pl.pallas_call(item_kernel, out_shape=jax.ShapeDtypeStruct((slots, outw),...  15.1 us
    all_to_all x1, starting transfers between devices, per_device(): lax.all_to_all(outgoing.reshape(peers, cap, outw), ('grp', 'rep'), split_...  11.5 us
    all_to_all x1, starting transfers between devices, per_device(): lax.all_to_all(slot_grads.reshape(peers, cap, outw), ('grp', 'rep'), spli...  6.26 us
    pallas_call x1, Pallas kernels, per_device(): pl.pallas_call(slot_kernel, out_shape=jax.ShapeDtypeStruct((slots, outw),...  5.89 us
  transfers between devices with their start and end apart: 2, of which 2 were waited for; matrix products, arithmetic and copies ran while one was open for 1% of the time, Pallas kernels for 10%

profile of v2, /device:TPU:1, one launch (start us, length us, event | category | flops | bytes accessed | tf_op | source)
XLA Modules:
  0.0 150.5 jit_solution(9605376892764872312)
XLA Ops:
  0.6 0.0 copy-start.2
  0.6 0.7 iota_compare_fusion
  1.4 0.1 lt.23
  1.5 0.8 copy.13
  2.3 0.1 squeeze.3
  2.4 0.6 broadcast_select_fusion.rows
  3.0 15.1 %items.1 = bf16[4096,128]{1,0:T(8,128)(2,1)} custom-call(s32[4096]{0:T(1024)} %broadcast_select_fusion.rows, bf16[4096,256]{1,0:T(8,128)(2,1)} %table.5, bf16[256,512]{1,0:T(8,128)(2,1)} %w1.5, bf16[512,128]{1,0:T(8,128)(2,1)} %w2.5), custom_call_target="tpu_custom_call" | custom-call | flops 1610612736 | bytes 4194304 | tf_op jit(solution)/shard_map/items/pallas_call | solution.py:345
  18.1 11.5 %all-to-all-start = ((bf16[128,32,128]{2,1,0:T(8,128)(2,1)}), bf16[128,32,128]{2,1,0:T(8,128)(2,1)S(1)}, u32[]{:S(2)}, u32[]{:S(2)}) async-start(bf16[128,32,128]{2,1,0:T(8,128)(2,1)} %bitcast.10), calls=%async_computation | async-start | bytes 2097152 | tf_op jit(solution)/shard_map/all_to_all | solution.py:355
  29.6 0.0 copy-done.2
  29.6 0.2 copy.14
  29.8 0.8 reshape.32.ids
  30.6 15.5 %users.1.queries = bf16[1024,128]{1,0:T(8,128)(2,1)} custom-call(s32[8192]{0:T(1024)} %reshape.32.ids, bf16[8192,256]{1,0:T(8,128)(2,1)} %table.3, bf16[256,512]{1,0:T(8,128)(2,1)} %w1.3, bf16[512,128]{1,0:T(8,128)(2,1)} %w2.3), custom_call_target="tpu_custom_call" | custom-call | flops 8589934592 | bytes 16777216 | tf_op jit(solution)/shard_map/users/pallas_call | solution.py:359
  46.2 2.3 %all-to-all-done = bf16[128,32,128]{2,1,0:T(8,128)(2,1)S(1)} async-done(((bf16[128,32,128]{2,1,0:T(8,128)(2,1)}), bf16[128,32,128]{2,1,0:T(8,128)(2,1)S(1)}, u32[]{:S(2)}, u32[]{:S(2)}) %all-to-all-start) | async-done | bytes 1048608 | tf_op jit(solution)/shard_map/all_to_all | solution.py:355
  48.5 0.0 copy-start.1
  48.5 1.0 copy-done.1
  49.5 42.0 %scores.1 = (f32[1024,128]{1,0:T(8,128)}, f32[1024,128]{1,0:T(8,128)}, f32[1,1024]{1,0:T(1,128)}) custom-call(s32[1024]{0:T(1024)} %pos_slot.3, s32[1024]{0:T(1024)} %bitcast.11, bf16[1024,128]{1,0:T(8,128)(2,1)} %users.1.queries, bf16[4096,128]{1,0:T(8,128)(2,1)} %bitcast.9), custom_call_target="tpu_custom_call" | custom-call | flops 4294967296 | bytes 4194304 | tf_op jit(solution)/shard_map/scores/pallas_call | solution.py:371
  91.5 5.9 %slot_sums.1 = bf16[4096,128]{1,0:T(8,128)(2,1)} custom-call(s32[1024]{0:T(1024)} %pos_slot.3, s32[1024]{0:T(1024)} %bitcast.12, f32[1024,128]{1,0:T(8,128)} %get-tuple-element.5.pos_grad, f32[1024,128]{1,0:T(8,128)} %get-tuple-element.6.neg_grad), custom_call_target="tpu_custom_call" | custom-call | tf_op jit(solution)/shard_map/slot_sums/pallas_call | solution.py:398
  97.3 6.3 %all-to-all-start.1 = ((bf16[128,32,128]{2,1,0:T(8,128)(2,1)}), bf16[128,32,128]{2,1,0:T(8,128)(2,1)S(1)}, u32[]{:S(2)}, u32[]{:S(2)}) async-start(bf16[128,32,128]{2,1,0:T(8,128)(2,1)} %bitcast.7), calls=%async_computation.1 | async-start | bytes 2097152 | tf_op jit(solution)/shard_map/all_to_all | solution.py:407
  103.6 0.0 copy-start.3
  103.6 18.9 %all-to-all-done.1 = bf16[128,32,128]{2,1,0:T(8,128)(2,1)S(1)} async-done(((bf16[128,32,128]{2,1,0:T(8,128)(2,1)}), bf16[128,32,128]{2,1,0:T(8,128)(2,1)S(1)}, u32[]{:S(2)}, u32[]{:S(2)}) %all-to-all-start.1) | async-done | bytes 1048608 | tf_op jit(solution)/shard_map/all_to_all | solution.py:407
  122.5 1.0 copy-done
  123.5 26.4 %row_grads.1 = f32[4096,256]{1,0:T(8,128)} custom-call(s32[4096]{0:T(1024)} %broadcast_select_fusion.rows, bf16[4096,128]{1,0:T(8,128)(2,1)} %bitcast.8, bf16[4096,256]{1,0:T(8,128)(2,1)} %table.5, bf16[256,512]{1,0:T(8,128)(2,1)} %w1.5, bf16[512,128]{1,0:T(8,128)(2,1)} %w2.5), custom_call_target="tpu_custom_call" | custom-call | tf_op jit(solution)/shard_map/row_grads/pallas_call | solution.py:411
  149.9 0.0 copy-done.3
  149.9 0.6 copy.16
  (1 shorter events, 0.0 us)
Async XLA Ops:
  0.6 29.0 %copy-start.2 = (s32[1024,8]{0,1:T(8,128)S(1)}, s32[1024,8]{0,1:T(8,128)}, u32[]{:S(2)}) copy-start(s32[1024,8]{0,1:T(8,128)} %param.16) | copy-start | bytes 98308
  18.1 30.4 %all-to-all-start = ((bf16[128,32,128]{2,1,0:T(8,128)(2,1)}), bf16[128,32,128]{2,1,0:T(8,128)(2,1)S(1)}, u32[]{:S(2)}, u32[]{:S(2)}) async-start(bf16[128,32,128]{2,1,0:T(8,128)(2,1)} %bitcast.10), calls=%async_computation | async-start | bytes 2097152 | tf_op jit(solution)/shard_map/all_to_all | solution.py:355
  48.5 1.0 copy-start.1
  97.3 25.2 %all-to-all-start.1 = ((bf16[128,32,128]{2,1,0:T(8,128)(2,1)}), bf16[128,32,128]{2,1,0:T(8,128)(2,1)S(1)}, u32[]{:S(2)}, u32[]{:S(2)}) async-start(bf16[128,32,128]{2,1,0:T(8,128)(2,1)} %bitcast.7), calls=%async_computation.1 | async-start | bytes 2097152 | tf_op jit(solution)/shard_map/all_to_all | solution.py:407
  103.6 46.3 %copy-start.3 = (f32[1,1024]{1,0:T(1,128)S(1)}, f32[1,1024]{1,0:T(1,128)}, u32[]{:S(2)}) copy-start(f32[1,1024]{1,0:T(1,128)} %get-tuple-element.7) | copy-start | bytes 12292
  122.5 1.0 copy-start

commit v3 on v0

v3 whole, which is shorter than its diff:
```python
import math

import jax
import jax.numpy as jnp
from jax import lax
from jax.experimental import pallas as pl
from jax.experimental.pallas import tpu as pltpu
from jax.sharding import PartitionSpec as P

LOGIT_SCALE = 20.0
NORM_EPS = 1e-06
LOG2E = math.log2(math.e)
MESH = pl.DeviceIdType.MESH
VMEM = pl.BlockSpec(memory_space=pltpu.VMEM)
SMEM = pl.BlockSpec(memory_space=pltpu.SMEM)
ANY = pl.BlockSpec(memory_space=pl.ANY)
F32, BF16 = jnp.float32, jnp.bfloat16
TILE = 1024
GROUPS = 8


def mm(a, b):
    return jnp.dot(a, b, preferred_element_type=F32)


def mm_t(a, b):
    return lax.dot_general(a, b, (((1,), (1,)), ((), ())), preferred_element_type=F32)


def tower(x, w1, w2):
    pre = mm(x, w1)
    sig = 0.5 + 0.5 * jnp.tanh(0.5 * pre)
    out = mm((pre * sig).astype(BF16), w2)
    inv = lax.rsqrt(jnp.sum(out * out, axis=-1, keepdims=True) + NORM_EPS)
    return pre, sig, inv, out * inv


def upright(row):
    return jnp.transpose(jnp.broadcast_to(row, (128, row.shape[1])))


def spread(at, grads):
    half = 2048
    low = jnp.where(at >= half, at - half, at)
    hot = jnp.where(
        lax.broadcasted_iota(jnp.int32, (half, at.shape[1]), 0) == low, 1.0, 0.0
    ).astype(BF16)
    upper = upright(at.astype(F32)) >= half
    grads = grads.astype(F32)
    both = jnp.concatenate(
        [jnp.where(upper, 0.0, grads), jnp.where(upper, grads, 0.0)], axis=1
    ).astype(BF16)
    return mm(hot, both)


def window_kernel(
    rows, pos_slot, neg_slot, ids, table, w1, w2, u1, u2, row_at, pos_at, neg_at, user_table,
    out, loss,
    ut, low, high, plow, phigh, unit, wide, send, recv, cols, group, pexp, nexp, scaled,
    sums_out, sums_in, rates, acc, back_send, back_recv,
    t_sem, o_sem, a_send, a_recv, b_send, b_recv, l_sem,
    q_send, q_recv, f_send, f_recv, s_send, s_recv, r_send, r_recv,
):
    n, users = table.shape[0], group.shape[1]
    cap = 32
    grp, rep = lax.axis_size("grp"), lax.axis_size("rep")
    peers = grp * rep
    chips = grp // 2
    g, r = lax.axis_index("grp"), lax.axis_index("rep")
    me = g * rep + r
    chip, core = g // 2, lax.rem(g, 2)

    def place(t):
        return (t // rep, lax.rem(t, rep))

    barrier = pltpu.get_barrier_semaphore()

    def greet(k, c):
        pl.semaphore_signal(
            barrier, inc=1, device_id=place(lax.rem(me + k, peers)), device_id_type=MESH
        )
        return c

    lax.fori_loop(1, peers, greet, 0)
    fetch = pltpu.make_async_copy(user_table, ut, t_sem)
    fetch.start()

    unit[pl.ds(n, 8), :] = jnp.zeros((8, unit.shape[1]), F32)

    def forward(i, c):
        at = pl.ds(pl.multiple_of(i * TILE, TILE), TILE)
        unit[at, :] = tower(table[at, :], w1[...], w2[...])[3]
        return c

    lax.fori_loop(0, n // TILE, forward, 0)
    pl.semaphore_wait(barrier, peers - 1)

    def span(t):
        return pl.ds(pl.multiple_of(t * cap, cap), cap)

    def gather_list(t):
        for j in range(cap):
            wide[pl.ds(t * cap + j, 1), :] = unit[pl.ds(rows[t * cap + j], 1), :]
        send[span(t), :] = wide[span(t), :].astype(BF16)

    def send_list(k, c):
        t = lax.rem(me + k, peers)
        gather_list(t)
        pltpu.make_async_remote_copy(
            src_ref=send.at[span(t), :], dst_ref=recv.at[span(me), :],
            send_sem=a_send, recv_sem=a_recv, device_id=place(t), device_id_type=MESH,
        ).start()
        return c

    lax.fori_loop(1, peers, send_list, 0)
    gather_list(me)
    keep = pltpu.make_async_copy(send.at[span(me), :], recv.at[span(me), :], l_sem)
    keep.start()

    fetch.wait()

    def widen(i, c):
        at = pl.ds(pl.multiple_of(i * 256, 256), 256)
        low[at, :] = ut[at, :128].astype(F32)
        high[at, :] = ut[at, 128:].astype(F32)
        return c

    lax.fori_loop(0, ut.shape[0] // 256, widen, 0)

    def pool(i, c):
        for k in range(8):
            b = i * 8 + k
            at = [pl.ds(ids[f, b], 1) for f in range(ids.shape[0])]
            lo = [low[a, :] for a in at]
            hi = [high[a, :] for a in at]
            while len(lo) > 1:
                lo = [x + y for x, y in zip(lo[::2], lo[1::2])]
                hi = [x + y for x, y in zip(hi[::2], hi[1::2])]
            plow[pl.ds(b, 1), :] = lo[0]
            phigh[pl.ds(b, 1), :] = hi[0]
        return c

    lax.fori_loop(0, users // 8, pool, 0)
    pooled = jnp.concatenate([plow[...], phigh[...]], axis=1).astype(BF16)
    group[0] = tower(pooled, u1[...], u2[...])[3].astype(BF16)

    far = sorted(range(1, chips), key=lambda k: (min(k, chips - k), k))
    names = [(0, 0), (0, 1)] + [(k, 0) for k in far] + [(k, 1) for k in far]
    slot_of = {name: i for i, name in enumerate(names)}

    def push(src, dst, ss, rs, k, flip):
        to = lax.rem(chip + k, chips) * 2 + (1 - core if flip else core)
        return pltpu.make_async_remote_copy(
            src_ref=src, dst_ref=dst, send_sem=ss, recv_sem=rs,
            device_id=(to, r), device_id_type=MESH,
        )

    f_copies = {0: push(group.at[0], group.at[1], f_send.at[0], f_recv.at[0], 0, 1)}
    q_copies = {}
    for k in far:
        s = slot_of[(k, 0)]
        q_copies[k] = push(group.at[0], group.at[s], q_send.at[k], q_recv.at[k], chips - k, 0)
        f_copies[k] = push(group.at[s], group.at[slot_of[(k, 1)]], f_send.at[k], f_recv.at[k], 0, 1)
        q_copies[k].start()
    f_copies[0].start()

    keep.wait()
    others = pl.ds(0, (peers - 1) * cap)
    pltpu.make_async_copy(send.at[others, :], recv.at[others, :], a_recv).wait()
    wide[...] = recv[...].astype(F32)

    def pick(i, c):
        for j in range(32):
            low[pl.ds(i * 32 + j, 1), :] = wide[pl.ds(neg_slot[i * 32 + j], 1), :]
        for j in range(32):
            low[pl.ds(users + i * 32 + j, 1), :] = wide[pl.ds(pos_slot[i * 32 + j], 1), :]
        return c

    lax.fori_loop(0, users // 32, pick, 0)
    cols[...] = low[pl.ds(0, 2 * users), :].astype(BF16)

    s = mm_t(cols[pl.ds(0, users), :], group[0])
    e = jnp.exp2(s * (LOGIT_SCALE * LOG2E))
    nexp[...] = e.astype(BF16)
    other = jnp.sum(e, axis=0, keepdims=True)
    s = mm_t(cols[pl.ds(users, users), :], group[0])
    hit = lax.broadcasted_iota(jnp.int32, s.shape, 0) == lax.broadcasted_iota(jnp.int32, s.shape, 1)
    e = jnp.where(hit, 0.0, jnp.exp2(s * (LOGIT_SCALE * LOG2E)))
    own_score = jnp.sum(jnp.where(hit, s, 0.0), axis=0, keepdims=True) * LOGIT_SCALE
    pexp[0] = e.astype(BF16)
    other = other + jnp.sum(e, axis=0, keepdims=True)

    s_copies = []

    def compute(first, last):
        def one(k, c):
            s = mm_t(cols[pl.ds(users, users), :], group[k])
            e = jnp.exp2(s * (LOGIT_SCALE * LOG2E))
            pexp[k] = e.astype(BF16)
            sums_out[k] = jnp.sum(e, axis=0, keepdims=True)
            return c

        lax.fori_loop(first, last, one, 0)
        for i in range(first, last):
            k, flip = names[i]
            b = slot_of[((chips - k) % chips, flip)]
            s_copies.append(push(sums_out.at[i], sums_in.at[b], s_send.at[i], s_recv.at[b], k, flip))
            s_copies[-1].start()

    f_copies[0].wait_recv()
    compute(1, 2)
    for k in far:
        q_copies[k].wait_recv()
        f_copies[k].start()
    compute(2, 1 + chips)
    for k in far:
        f_copies[k].wait_recv()
    compute(1 + chips, grp)
    for c in s_copies:
        c.wait_recv()

    for k in range(1, grp):
        other = other + sums_in[k]
    total = other + jnp.exp2(own_score * LOG2E)
    loss[...] = jnp.log(total) - own_score
    rate = LOGIT_SCALE / total
    rates[0] = rate
    r_copies = []
    for i in range(1, grp):
        k, flip = names[i]
        b = slot_of[((chips - k) % chips, flip)]
        r_copies.append(push(rates.at[0], rates.at[b], r_send.at[i], r_recv.at[b], k, flip))
        r_copies[-1].start()

    scaled[0] = (group[0].astype(F32) * upright(rate)).astype(BF16)
    acc[...] = spread(neg_at[...], mm(nexp[...], scaled[0]))
    own = group[0].astype(F32) * upright(rate * other)
    for c in r_copies:
        c.wait_recv()

    def scale(k, c):
        scaled[k] = (group[k].astype(F32) * upright(rates[k])).astype(BF16)
        return c

    lax.fori_loop(1, grp, scale, 0)
    grads = mm(pexp[0], scaled[0]) - own
    for k in range(1, grp):
        grads = grads + mm(pexp[k], scaled[k])
    total_grads = acc[...] + spread(pos_at[...], grads)
    half = n // 2
    back_send[pl.ds(0, half), :] = total_grads[:, :128].astype(BF16)
    back_send[pl.ds(half, half), :] = total_grads[:, 128:].astype(BF16)

    per = peers // GROUPS

    def send_back(k, c):
        t = lax.rem(me + k, peers)
        pltpu.make_async_remote_copy(
            src_ref=back_send.at[span(t), :], dst_ref=back_recv.at[span(me), :],
            send_sem=b_send, recv_sem=b_recv.at[me // per], device_id=place(t), device_id_type=MESH,
        ).start()
        return c

    lax.fori_loop(1, peers, send_back, 0)
    keep = pltpu.make_async_copy(
        back_send.at[span(me), :], back_recv.at[span(me), :], b_recv.at[me // per]
    )
    keep.start()

    def slope(i, c):
        at = pl.ds(pl.multiple_of(i * TILE, TILE), TILE)
        pre, sig, inv, _ = tower(table[at, :], w1[...], w2[...])
        pexp[i, :, :512] = (sig * (1.0 + pre * (1.0 - sig)) * inv).astype(BF16)
        return c

    lax.fori_loop(0, n // TILE, slope, 0)

    acc[...] = jnp.zeros(acc.shape, F32)

    def arrive(i, c):
        b = lax.rem(me // per + 2 * GROUPS - 1 - i, GROUPS)
        at = pl.ds(pl.multiple_of(b * (per * cap), per * cap), per * cap)
        pltpu.make_async_copy(back_send.at[at, :], back_recv.at[at, :], b_recv.at[b]).wait()
        acc[...] = acc[...] + spread(row_at[pl.ds(b, 1), :], back_recv[at, :])
        return c

    lax.fori_loop(0, GROUPS, arrive, 0)

    o_copies = []
    for i in range(n // TILE):
        at = pl.ds(i * TILE, TILE)
        side = i * TILE // half * 128
        grad = acc[pl.ds(i * TILE % half, TILE), side:side + 128]
        u = unit[at, :]
        d_out = (grad - u * jnp.sum(u * grad, axis=-1, keepdims=True)).astype(BF16)
        d_pre = (mm_t(d_out, w2[...]) * pexp[i, :, :512].astype(F32)).astype(BF16)
        d_row = mm_t(d_pre, w1[...])
        low[at, :] = d_row[:, :128]
        high[at, :] = d_row[:, 128:]
        o_copies += [
            pltpu.make_async_copy(low.at[at, :], out.at[at, pl.ds(0, 128)], o_sem.at[2 * i]),
            pltpu.make_async_copy(high.at[at, :], out.at[at, pl.ds(128, 128)], o_sem.at[2 * i + 1]),
        ]
        o_copies[-2].start()
        o_copies[-1].start()

    for c in list(q_copies.values()) + list(f_copies.values()) + s_copies + r_copies:
        c.wait_send()
    pltpu.make_async_copy(send.at[others, :], recv.at[others, :], a_send).wait()
    pltpu.make_async_copy(back_send.at[others, :], back_recv.at[others, :], b_send).wait()
    for c in o_copies:
        c.wait()


def per_device(
    item_table, send_rows, send_count, pos_slot, neg_slot, user_ids,
    user_table, item_w1, item_w2, user_w1, user_w2,
):
    peers, cap = send_rows.shape[1:]
    slots = peers * cap
    n, users = item_table.shape[0], pos_slot.shape[0]
    vocab, outw = user_table.shape[0], item_w2.shape[1]
    grp = lax.axis_size("grp")
    chips = grp // 2
    live = jnp.arange(cap, dtype=jnp.int32)[:, None] < send_count
    rows = jnp.where(live, send_rows[0].T, n).T.reshape(-1)
    neg = neg_slot.reshape(-1)

    dma = pltpu.SemaphoreType.DMA
    vm = pltpu.VMEM
    table_grad, loss = pl.pallas_call(
        window_kernel,
        out_shape=[
            jax.ShapeDtypeStruct(item_table.shape, F32),
            jax.ShapeDtypeStruct((1, users), F32),
        ],
        in_specs=[SMEM] * 4 + [VMEM] * 8 + [ANY],
        out_specs=[ANY, VMEM],
        scratch_shapes=[
            vm(user_table.shape, BF16), vm((vocab, 128), F32), vm((vocab, 128), F32),
            vm((users, 128), F32), vm((users, 128), F32),
            vm((n + 8, outw), F32), vm((slots, outw), F32),
            vm((slots, outw), BF16), vm((slots, outw), BF16),
            vm((2 * users, outw), BF16),
            vm((grp, users, outw), BF16), vm((grp, users, users), BF16), vm((users, users), BF16),
            vm((grp, users, outw), BF16),
            vm((grp, 1, users), F32), vm((grp, 1, users), F32), vm((grp, 1, users), F32),
            vm((n // 2, 2 * outw), F32),
            vm((slots, outw), BF16), vm((slots, outw), BF16),
            dma, dma((2 * n // TILE,)), dma, dma, dma, dma((GROUPS,)), dma,
            dma((chips,)), dma((chips,)), dma((chips,)), dma((chips,)),
            dma((grp,)), dma((grp,)), dma((grp,)), dma((grp,)),
        ],
        compiler_params=pltpu.CompilerParams(
            collective_id=0, has_side_effects=True, vmem_limit_bytes=60 * 2**20
        ),
        cost_estimate=pl.CostEstimate(flops=2**34, bytes_accessed=2**24, transcendentals=2**24),
        name="window",
    )(
        rows, pos_slot, neg, user_ids.T, item_table, item_w1, item_w2, user_w1, user_w2,
        rows.reshape(GROUPS, -1), pos_slot.reshape(1, -1), neg_slot, user_table,
    )
    return table_grad, loss.reshape(-1)


def solution(mesh):
    return jax.shard_map(
        per_device,
        mesh=mesh,
        in_specs=(
            P(("grp", "rep"), None),
            P(("grp", "rep"), None, None),
            P(("grp", "rep"), None),
            P(("grp", "rep")),
            P(("grp", "rep"), None),
            P(("grp", "rep"), None),
            P(), P(), P(), P(), P(),
        ),
        out_specs=(P(("grp", "rep"), None), P(("grp", "rep"))),
        check_vma=False,
    )
```

time: 309 us -> 105 us (0.34)
  Pallas kernels: 0 us -> 93.7 us
  waiting for transfers between devices: 82.5 us -> 0 us
  local copies, waits for them, and re-layouts: 80.9 us -> 6.99 us
  other arithmetic: 55.6 us -> 3.27 us
  matrix products: 52.1 us -> 0 us
  starting transfers between devices: 22.1 us -> 0 us
  between operations: 14.4 us -> 0.67 us
    pallas_call x0 -> x1, Pallas kernels: none -> 93.7 us  [per_device(): pl.pallas_call(window_kernel, out_shape=[jax.ShapeDtypeStruct(item_table....]
    gather x5 -> x0, local copies, waits for them, and re-layouts: 76 us -> none  [the longest x1 34.1 us: per_device(): user_table[user_ids].astype(jnp.float32)]
    all_to_all x2 -> x0, waiting for transfers between devices: 58.3 us -> none  [the longest x1 29.4 us: per_device(): lax.all_to_all(outgoing, ('grp', 'rep'), split_axis=0, concat_axis=0, til...]
    dot_general x8 -> x0, matrix products: 52.1 us -> none  [the longest x1 18.1 us: per_device(): jnp.einsum('bc,bo->co', slope_pos, queries, preferred_element_type=jnp.fl...]
    scatter-add x3 -> x0, other arithmetic: 38.8 us -> none  [the longest x1 25.1 us: per_device(): table_grad.at[row_ids.reshape(-1)].add(values.reshape(-1, emb_width))]
    reduce_scatter x1 -> x0, waiting for transfers between devices: 24.1 us -> none  [per_device(): lax.psum_scatter(jnp.einsum('bc,bo->co', slope_pos, queries, preferred_el...]
    all_to_all x2 -> x0, starting transfers between devices: 22 us -> none  [the longest x1 11.5 us: per_device(): lax.all_to_all(outgoing, ('grp', 'rep'), split_axis=0, concat_axis=0, til...]
    reduce_sum x2 -> x0, other arithmetic: 7.69 us -> none  [the longest x1 5.03 us: per_device(): jnp.sum(user_table[user_ids].astype(jnp.float32), axis=1)]
  transfers between devices with their start and end apart: 4 -> 0, of which waited for: 3 -> 0; matrix products, arithmetic and copies ran while one was open for 16% -> 0% of each run, Pallas kernels for 0% -> 0%
where the time goes in v3:
time: 105 us
  Pallas kernels  93.7 us (89%)
  local copies, waits for them, and re-layouts  6.99 us (7%)
  other arithmetic  3.27 us (3%)
    pallas_call x1, Pallas kernels, per_device(): pl.pallas_call(window_kernel, out_shape=[jax.ShapeDtypeStruct(item_table....  93.7 us
    unnamed x6, local copies, waits for them, and re-layouts  6.4 us

profile of v3, /device:TPU:1, one launch (start us, length us, event | category | flops | bytes accessed | tf_op | source)
XLA Modules:
  0.0 104.6 jit_solution(7729019705408747979)
XLA Ops:
  0.6 0.5 broadcast.15
  1.1 1.3 %reduce.3 = s32[128]{0:T(128)S(1)} reduce(s32[1,128]{1,0:T(1,128)} %param.13, s32[]{:T(128)} %broadcast.15), dimensions={0}, to_apply=%param.13.reduce_sub_computation.3 | reduce | bytes 1028 | tf_op args[2]
  2.5 0.1 lt.43
  2.5 0.1 lt.41
  2.6 0.7 iota_compare_fusion
  3.4 0.1 lt.39
  3.5 0.1 lt.44
  3.5 0.1 lt.45
  3.6 0.8 copy.14
  4.5 0.1 squeeze.6
  4.6 0.1 squeeze.5
  4.6 0.6 compare_select_fusion.row_at
  5.2 0.6 broadcast_select_fusion.rows
  5.8 93.7 %window.1 = (f32[4096,256]{1,0:T(8,128)}, f32[1,1024]{1,0:T(1,128)}) custom-call(s32[4096]{0:T(1024)} %broadcast_select_fusion.rows, s32[1024]{0:T(1024)} %pos_slot.1, s32[1024]{0:T(1024)} %bitcast.9, s32[8,1024]{1,0:T(8,128)} %bitcast.7, bf16[4096,256]{1,0:T(8,128)(2,1)} %table.1, bf16[256,512]{1,0:T(8,128)(2,1)} %w1.1, bf16[512,128]{1,0:T(8,128)(2,1)} %w2.1, ...), custom_call_target="tpu_custom_call" | custom-call | flops 17179869184 | bytes 16777216 | tf_op jit(solution)/shard_map/window/pallas_call | solution.py:331
  99.5 0.0 copy-start
  99.5 4.5 %copy.18 = f32[4096,256]{1,0:T(8,128)} copy(f32[4096,256]{1,0:T(8,128)} %get-tuple-element.8) | data formatting | bytes 8388608
  104.0 0.0 copy-done
  104.0 0.6 copy.19
  (1 shorter events, 0.0 us)
Async XLA Ops:
  99.5 4.5 %copy-start = (f32[1,1024]{1,0:T(1,128)S(1)}, f32[1,1024]{1,0:T(1,128)}, u32[]{:S(2)}) copy-start(f32[1,1024]{1,0:T(1,128)} %get-tuple-element.5) | copy-start | bytes 12292

commit v4 on v3

--- a/solution.py
+++ b/solution.py
@@ -54,11 +54,11 @@
 
 
 def window_kernel(
-    rows, pos_slot, neg_slot, ids, table, w1, w2, u1, u2, row_at, pos_at, neg_at, user_table,
-    out, loss,
+    pos_slot, neg_slot, ids, lists, counts, table, w1, w2, u1, u2, pos_at, neg_at, user_table,
+    d_out, slopes, loss,
     ut, low, high, plow, phigh, unit, wide, send, recv, cols, group, pexp, nexp, scaled,
-    sums_out, sums_in, rates, acc, back_send, back_recv,
-    t_sem, o_sem, a_send, a_recv, b_send, b_recv, l_sem,
+    sums_out, sums_in, rates, acc, back_send, back_recv, live_rows, rows, row_at,
+    t_sem, i_sem, o_sem, a_send, a_recv, b_send, b_recv, l_sem,
     q_send, q_recv, f_send, f_recv, s_send, s_recv, r_send, r_recv,
 ):
     n, users = table.shape[0], group.shape[1]
@@ -85,38 +85,12 @@
     fetch = pltpu.make_async_copy(user_table, ut, t_sem)
     fetch.start()
 
-    unit[pl.ds(n, 8), :] = jnp.zeros((8, unit.shape[1]), F32)
-
-    def forward(i, c):
-        at = pl.ds(pl.multiple_of(i * TILE, TILE), TILE)
-        unit[at, :] = tower(table[at, :], w1[...], w2[...])[3]
-        return c
-
-    lax.fori_loop(0, n // TILE, forward, 0)
-    pl.semaphore_wait(barrier, peers - 1)
-
-    def span(t):
-        return pl.ds(pl.multiple_of(t * cap, cap), cap)
-
-    def gather_list(t):
-        for j in range(cap):
-            wide[pl.ds(t * cap + j, 1), :] = unit[pl.ds(rows[t * cap + j], 1), :]
-        send[span(t), :] = wide[span(t), :].astype(BF16)
-
-    def send_list(k, c):
-        t = lax.rem(me + k, peers)
-        gather_list(t)
-        pltpu.make_async_remote_copy(
-            src_ref=send.at[span(t), :], dst_ref=recv.at[span(me), :],
-            send_sem=a_send, recv_sem=a_recv, device_id=place(t), device_id_type=MESH,
-        ).start()
-        return c
-
-    lax.fori_loop(1, peers, send_list, 0)
-    gather_list(me)
-    keep = pltpu.make_async_copy(send.at[span(me), :], recv.at[span(me), :], l_sem)
-    keep.start()
-
+    live = lax.broadcasted_iota(jnp.int32, lists.shape, 0) < counts[...]
+    live_rows[...] = jnp.where(live, lists[...], n)
+    index = pltpu.make_async_copy(live_rows, rows, i_sem)
+    index.start()
+
+    o_copies = []
     fetch.wait()
 
     def widen(i, c):
@@ -161,8 +135,72 @@
         s = slot_of[(k, 0)]
         q_copies[k] = push(group.at[0], group.at[s], q_send.at[k], q_recv.at[k], chips - k, 0)
         f_copies[k] = push(group.at[s], group.at[slot_of[(k, 1)]], f_send.at[k], f_recv.at[k], 0, 1)
+
+    pl.semaphore_wait(barrier, peers - 1)
+    for k in far:
         q_copies[k].start()
     f_copies[0].start()
+
+    unit[pl.ds(n, 8), :] = jnp.zeros((8, unit.shape[1]), F32)
+
+    def forward(i, c):
+        at = pl.ds(pl.multiple_of(i * TILE, TILE), TILE)
+        unit[at, :] = tower(table[at, :], w1[...], w2[...])[3]
+        return c
+
+    lax.fori_loop(0, n // TILE, forward, 0)
+
+    def span(t):
+        return pl.ds(pl.multiple_of(t * cap, cap), cap)
+
+    def gather_list(t):
+        for j in range(cap):
+            wide[pl.ds(t * cap + j, 1), :] = unit[pl.ds(rows[j, t], 1), :]
+        send[span(t), :] = wide[span(t), :].astype(BF16)
+
+    def send_list(k, c):
+        t = lax.rem(me + k, peers)
+        gather_list(t)
+        pltpu.make_async_remote_copy(
+            src_ref=send.at[span(t), :], dst_ref=recv.at[span(me), :],
+            send_sem=a_send, recv_sem=a_recv, device_id=place(t), device_id_type=MESH,
+        ).start()
+        return c
+
+    index.wait()
+    lax.fori_loop(1, peers, send_list, 0)
+    gather_list(me)
+    keep = pltpu.make_async_copy(send.at[span(me), :], recv.at[span(me), :], l_sem)
+    keep.start()
+    for k in far:
+        q_copies[k].wait_recv()
+        f_copies[k].start()
+
+    for i in range(n // TILE):
+        at = pl.ds(i * TILE, TILE)
+        pre, sig, inv, _ = tower(table[at, :], w1[...], w2[...])
+        pexp[i, :, :512] = (sig * (1.0 + pre * (1.0 - sig)) * inv).astype(BF16)
+        o_copies.append(
+            pltpu.make_async_copy(pexp.at[i, :, pl.ds(0, 512)], slopes.at[at, :], o_sem.at[i])
+        )
+        o_copies[-1].start()
+
+    low_part = jnp.transpose(live_rows[...].astype(F32))
+    high_part = jnp.floor(low_part * (1.0 / 64.0))
+    low_part = low_part - 64.0 * high_part
+    width = peers // GROUPS * cap
+    tiled = (
+        lax.broadcasted_iota(jnp.int32, (cap, width), 0)
+        == lax.rem(lax.broadcasted_iota(jnp.int32, (cap, width), 1), cap)
+    ).astype(F32).astype(BF16)
+    along = 64.0 * mm(high_part.astype(BF16), tiled) + mm(low_part.astype(BF16), tiled)
+    mine = lax.rem(
+        lax.broadcasted_iota(jnp.int32, along.shape, 0), peers // GROUPS
+    ) == lax.broadcasted_iota(jnp.int32, along.shape, 1) // cap
+    along = jnp.where(mine, along, 0.0)
+    for b in range(GROUPS):
+        part = along[b * (peers // GROUPS):(b + 1) * (peers // GROUPS), :]
+        row_at[b:b + 1, :] = jnp.sum(part, axis=0, keepdims=True).astype(jnp.int32)
 
     keep.wait()
     others = pl.ds(0, (peers - 1) * cap)
@@ -178,6 +216,30 @@
 
     lax.fori_loop(0, users // 32, pick, 0)
     cols[...] = low[pl.ds(0, 2 * users), :].astype(BF16)
+
+    for c in o_copies:
+        c.wait()
+    s_copies = []
+
+    def compute(first, last):
+        def one(k, c):
+            s = mm_t(cols[pl.ds(users, users), :], group[k])
+            e = jnp.exp2(s * (LOGIT_SCALE * LOG2E))
+            pexp[k] = e.astype(BF16)
+            sums_out[k] = jnp.sum(e, axis=0, keepdims=True)
+            return c
+
+        lax.fori_loop(first, last, one, 0)
+        for i in range(first, last):
+            k, flip = names[i]
+            b = slot_of[((chips - k) % chips, flip)]
+            s_copies.append(push(sums_out.at[i], sums_in.at[b], s_send.at[i], s_recv.at[b], k, flip))
+            s_copies[-1].start()
+
+    for c in f_copies.values():
+        c.wait_recv()
+    compute(1, 5)
+    compute(5, grp)
 
     s = mm_t(cols[pl.ds(0, users), :], group[0])
     e = jnp.exp2(s * (LOGIT_SCALE * LOG2E))
@@ -190,32 +252,6 @@
     pexp[0] = e.astype(BF16)
     other = other + jnp.sum(e, axis=0, keepdims=True)
 
-    s_copies = []
-
-    def compute(first, last):
-        def one(k, c):
-            s = mm_t(cols[pl.ds(users, users), :], group[k])
-            e = jnp.exp2(s * (LOGIT_SCALE * LOG2E))
-            pexp[k] = e.astype(BF16)
-            sums_out[k] = jnp.sum(e, axis=0, keepdims=True)
-            return c
-
-        lax.fori_loop(first, last, one, 0)
-        for i in range(first, last):
-            k, flip = names[i]
-            b = slot_of[((chips - k) % chips, flip)]
-            s_copies.append(push(sums_out.at[i], sums_in.at[b], s_send.at[i], s_recv.at[b], k, flip))
-            s_copies[-1].start()
-
-    f_copies[0].wait_recv()
-    compute(1, 2)
-    for k in far:
-        q_copies[k].wait_recv()
-        f_copies[k].start()
-    compute(2, 1 + chips)
-    for k in far:
-        f_copies[k].wait_recv()
-    compute(1 + chips, grp)
     for c in s_copies:
         c.wait_recv()
 
@@ -267,14 +303,6 @@
     )
     keep.start()
 
-    def slope(i, c):
-        at = pl.ds(pl.multiple_of(i * TILE, TILE), TILE)
-        pre, sig, inv, _ = tower(table[at, :], w1[...], w2[...])
-        pexp[i, :, :512] = (sig * (1.0 + pre * (1.0 - sig)) * inv).astype(BF16)
-        return c
-
-    lax.fori_loop(0, n // TILE, slope, 0)
-
     acc[...] = jnp.zeros(acc.shape, F32)
 
     def arrive(i, c):
@@ -286,30 +314,22 @@
 
     lax.fori_loop(0, GROUPS, arrive, 0)
 
-    o_copies = []
     for i in range(n // TILE):
         at = pl.ds(i * TILE, TILE)
         side = i * TILE // half * 128
         grad = acc[pl.ds(i * TILE % half, TILE), side:side + 128]
         u = unit[at, :]
-        d_out = (grad - u * jnp.sum(u * grad, axis=-1, keepdims=True)).astype(BF16)
-        d_pre = (mm_t(d_out, w2[...]) * pexp[i, :, :512].astype(F32)).astype(BF16)
-        d_row = mm_t(d_pre, w1[...])
-        low[at, :] = d_row[:, :128]
-        high[at, :] = d_row[:, 128:]
-        o_copies += [
-            pltpu.make_async_copy(low.at[at, :], out.at[at, pl.ds(0, 128)], o_sem.at[2 * i]),
-            pltpu.make_async_copy(high.at[at, :], out.at[at, pl.ds(128, 128)], o_sem.at[2 * i + 1]),
-        ]
-        o_copies[-2].start()
-        o_copies[-1].start()
+        d_out[at, :] = (grad - u * jnp.sum(u * grad, axis=-1, keepdims=True)).astype(BF16)
 
     for c in list(q_copies.values()) + list(f_copies.values()) + s_copies + r_copies:
         c.wait_send()
     pltpu.make_async_copy(send.at[others, :], recv.at[others, :], a_send).wait()
     pltpu.make_async_copy(back_send.at[others, :], back_recv.at[others, :], b_send).wait()
-    for c in o_copies:
-        c.wait()
+
+
+def row_kernel(d_out, slopes, w1, w2, out):
+    d_pre = (mm_t(d_out[...], w2[...]) * slopes[...].astype(F32)).astype(BF16)
+    out[...] = mm_t(d_pre, w1[...])
 
 
 def per_device(
@@ -322,20 +342,19 @@
     vocab, outw = user_table.shape[0], item_w2.shape[1]
     grp = lax.axis_size("grp")
     chips = grp // 2
-    live = jnp.arange(cap, dtype=jnp.int32)[:, None] < send_count
-    rows = jnp.where(live, send_rows[0].T, n).T.reshape(-1)
     neg = neg_slot.reshape(-1)
 
     dma = pltpu.SemaphoreType.DMA
     vm = pltpu.VMEM
-    table_grad, loss = pl.pallas_call(
+    d_out, slopes, loss = pl.pallas_call(
         window_kernel,
         out_shape=[
-            jax.ShapeDtypeStruct(item_table.shape, F32),
+            jax.ShapeDtypeStruct((n, outw), BF16),
+            jax.ShapeDtypeStruct((n, item_w1.shape[1]), BF16),
             jax.ShapeDtypeStruct((1, users), F32),
         ],
-        in_specs=[SMEM] * 4 + [VMEM] * 8 + [ANY],
-        out_specs=[ANY, VMEM],
+        in_specs=[SMEM] * 3 + [VMEM] * 9 + [ANY],
+        out_specs=[VMEM, ANY, VMEM],
         scratch_shapes=[
             vm(user_table.shape, BF16), vm((vocab, 128), F32), vm((vocab, 128), F32),
             vm((users, 128), F32), vm((users, 128), F32),
@@ -347,7 +366,9 @@
             vm((grp, 1, users), F32), vm((grp, 1, users), F32), vm((grp, 1, users), F32),
             vm((n // 2, 2 * outw), F32),
             vm((slots, outw), BF16), vm((slots, outw), BF16),
-            dma, dma((2 * n // TILE,)), dma, dma, dma, dma((GROUPS,)), dma,
+            vm((cap, peers), jnp.int32), pltpu.SMEM((cap, peers), jnp.int32),
+            vm((GROUPS, slots // GROUPS), jnp.int32),
+            dma, dma, dma((n // TILE,)), dma, dma, dma, dma((GROUPS,)), dma,
             dma((chips,)), dma((chips,)), dma((chips,)), dma((chips,)),
             dma((grp,)), dma((grp,)), dma((grp,)), dma((grp,)),
         ],
@@ -357,9 +378,24 @@
         cost_estimate=pl.CostEstimate(flops=2**34, bytes_accessed=2**24, transcendentals=2**24),
         name="window",
     )(
-        rows, pos_slot, neg, user_ids.T, item_table, item_w1, item_w2, user_w1, user_w2,
-        rows.reshape(GROUPS, -1), pos_slot.reshape(1, -1), neg_slot, user_table,
+        pos_slot, neg, user_ids.T, send_rows[0].T, send_count, item_table, item_w1, item_w2,
+        user_w1, user_w2, pos_slot.reshape(1, -1), neg_slot, user_table,
     )
+    block = 512
+    table_grad = pl.pallas_call(
+        row_kernel,
+        out_shape=jax.ShapeDtypeStruct(item_table.shape, F32),
+        grid=(n // block,),
+        in_specs=[
+            pl.BlockSpec((block, outw), lambda i: (i, 0)),
+            pl.BlockSpec((block, item_w1.shape[1]), lambda i: (i, 0)),
+            pl.BlockSpec(item_w1.shape, lambda i: (0, 0)),
+            pl.BlockSpec(item_w2.shape, lambda i: (0, 0)),
+        ],
+        out_specs=pl.BlockSpec((block, item_table.shape[1]), lambda i: (i, 0)),
+        compiler_params=pltpu.CompilerParams(vmem_limit_bytes=32 * 2**20),
+        name="row_grads",
+    )(d_out, slopes, item_w1, item_w2)
     return table_grad, loss.reshape(-1)
 
 

time: 105 us -> 110 us (1.048)
  Pallas kernels: 93.7 us -> 105 us
  other arithmetic: 3.27 us -> 0 us
  local copies, waits for them, and re-layouts: 6.99 us -> 4.01 us
    pallas_call x1 -> x2, Pallas kernels: 93.7 us -> 105 us  [the longest x1 99.4 us: per_device(): pl.pallas_call(window_kernel, out_shape=[jax.ShapeDtypeStruct((n, outw),...]
    unnamed x6 -> x11, local copies, waits for them, and re-layouts: 6.4 us -> 4.01 us
    unnamed x1 -> x0, other arithmetic: 1.32 us -> none
    select_n x2 -> x0, other arithmetic: 1.21 us -> none  [per_device(): rows = jnp.where(live, send_rows[0].T, n).T.reshape(-1)]
where the time goes in v4:
time: 110 us; the launch traced here: 109 us
  Pallas kernels  105 us (95%)
  local copies, waits for them, and re-layouts  4.01 us (4%)
    pallas_call x1, Pallas kernels, per_device(): pl.pallas_call(window_kernel, out_shape=[jax.ShapeDtypeStruct((n, outw),...  99.4 us
    pallas_call x1, Pallas kernels, per_device(): pl.pallas_call(row_kernel, out_shape=jax.ShapeDtypeStruct(item_table.shap...  5.36 us
    unnamed x11, local copies, waits for them, and re-layouts  4.01 us

profile of v4, /device:TPU:1, one launch (start us, length us, event | category | flops | bytes accessed | tf_op | source)
XLA Modules:
  0.0 109.5 jit_solution(6964064347339041175)
XLA Ops:
  0.6 0.0 copy-start.2
  0.6 0.0 copy-start.3
  0.7 99.4 %window.1 = (bf16[4096,128]{1,0:T(8,128)(2,1)}, bf16[4096,512]{1,0:T(8,128)(2,1)}, f32[1,1024]{1,0:T(1,128)}) custom-call(s32[1024]{0:T(1024)} %pos_slot.1, s32[1024]{0:T(1024)} %bitcast.11, s32[8,1024]{1,0:T(8,128)} %bitcast.8, s32[32,128]{1,0:T(8,128)} %bitcast.9, s32[1,128]{1,0:T(1,128)} %counts.1, bf16[4096,256]{1,0:T(8,128)(2,1)} %table.1, ...), custom_call_target="tpu_custom_call" | custom-call | flops 17179869184 | bytes 16777216 | tf_op jit(solution)/shard_map/window/pallas_call | solution.py:349
  100.1 0.0 copy-done.2
  100.1 0.0 copy-done.3
  100.1 0.0 copy-start
  100.1 2.2 %copy-done = bf16[4096,512]{1,0:T(8,128)(2,1)S(1)} copy-done((bf16[4096,512]{1,0:T(8,128)(2,1)S(1)}, bf16[4096,512]{1,0:T(8,128)(2,1)}, u32[]{:S(2)}) %copy-start) | copy-done | bytes 4194328
  102.3 0.0 copy-start.1
  102.3 1.2 %copy-done.1 = bf16[4096,128]{1,0:T(8,128)(2,1)S(1)} copy-done((bf16[4096,128]{1,0:T(8,128)(2,1)S(1)}, bf16[4096,128]{1,0:T(8,128)(2,1)}, u32[]{:S(2)}) %copy-start.1) | copy-done | bytes 1048600
  103.5 0.0 copy-start.4
  103.5 5.4 %row_grads.1 = f32[4096,256]{1,0:T(8,128)} custom-call(bf16[4096,128]{1,0:T(8,128)(2,1)S(1)} %copy-done.1, bf16[4096,512]{1,0:T(8,128)(2,1)S(1)} %copy-done, bf16[256,512]{1,0:T(8,128)(2,1)S(1)} %copy-done.2, bf16[512,128]{1,0:T(8,128)(2,1)S(1)} %copy-done.3), custom_call_target="tpu_custom_call" | custom-call | tf_op jit(solution)/shard_map/row_grads/pallas_call | solution.py:385
  108.9 0.0 copy-done.4
  108.9 0.6 copy.14
Async XLA Ops:
  0.6 99.4 %copy-start.2 = (bf16[256,512]{1,0:T(8,128)(2,1)S(1)}, bf16[256,512]{1,0:T(8,128)(2,1)}, u32[]{:S(2)}) copy-start(bf16[256,512]{1,0:T(8,128)(2,1)} %w1.3) | copy-start | bytes 786436
  0.6 99.4 %copy-start.3 = (bf16[512,128]{1,0:T(8,128)(2,1)S(1)}, bf16[512,128]{1,0:T(8,128)(2,1)}, u32[]{:S(2)}) copy-start(bf16[512,128]{1,0:T(8,128)(2,1)} %w2.3) | copy-start | bytes 393220
  100.1 2.2 %copy-start = (bf16[4096,512]{1,0:T(8,128)(2,1)S(1)}, bf16[4096,512]{1,0:T(8,128)(2,1)}, u32[]{:S(2)}) copy-start(bf16[4096,512]{1,0:T(8,128)(2,1)} %get-tuple-element.6.slopes) | copy-start | bytes 12582916
  102.3 1.2 %copy-start.1 = (bf16[4096,128]{1,0:T(8,128)(2,1)S(1)}, bf16[4096,128]{1,0:T(8,128)(2,1)}, u32[]{:S(2)}) copy-start(bf16[4096,128]{1,0:T(8,128)(2,1)} %get-tuple-element.5.d_out) | copy-start | bytes 3145732
  103.5 5.4 %copy-start.4 = (f32[1,1024]{1,0:T(1,128)S(1)}, f32[1,1024]{1,0:T(1,128)}, u32[]{:S(2)}) copy-start(f32[1,1024]{1,0:T(1,128)} %get-tuple-element.7) | copy-start | bytes 12292

commit v5 on v4

--- a/solution.py
+++ b/solution.py
@@ -17,6 +17,7 @@
 F32, BF16 = jnp.float32, jnp.bfloat16
 TILE = 1024
 GROUPS = 8
+PARTS = 4
 
 
 def mm(a, b):
@@ -90,7 +91,15 @@
     index = pltpu.make_async_copy(live_rows, rows, i_sem)
     index.start()
 
-    o_copies = []
+    unit[pl.ds(n, 8), :] = jnp.zeros((8, unit.shape[1]), F32)
+
+    def forward(i, c):
+        at = pl.ds(pl.multiple_of(i * TILE, TILE), TILE)
+        unit[at, :] = tower(table[at, :], w1[...], w2[...])[3]
+        return c
+
+    lax.fori_loop(0, n // TILE, forward, 0)
+
     fetch.wait()
 
     def widen(i, c):
@@ -100,11 +109,37 @@
         return c
 
     lax.fori_loop(0, ut.shape[0] // 256, widen, 0)
+    pl.semaphore_wait(barrier, peers - 1)
+
+    def span(t):
+        return pl.ds(pl.multiple_of(t * cap, cap), cap)
+
+    def gather_list(t):
+        for j in range(cap):
+            wide[pl.ds(t * cap + j, 1), :] = unit[pl.ds(rows[j, t], 1), :]
+        send[span(t), :] = wide[span(t), :].astype(BF16)
+
+    def send_list(k, c):
+        t = lax.rem(me + k, peers)
+        gather_list(t)
+        pltpu.make_async_remote_copy(
+            src_ref=send.at[span(t), :], dst_ref=recv.at[span(me), :],
+            send_sem=a_send, recv_sem=a_recv, device_id=place(t), device_id_type=MESH,
+        ).start()
+        return c
+
+    index.wait()
+    lax.fori_loop(1, peers, send_list, 0)
+    gather_list(me)
+    keep = pltpu.make_async_copy(send.at[span(me), :], recv.at[span(me), :], l_sem)
+    keep.start()
+
+    feat = ids.shape[0] // users
 
     def pool(i, c):
         for k in range(8):
             b = i * 8 + k
-            at = [pl.ds(ids[f, b], 1) for f in range(ids.shape[0])]
+            at = [pl.ds(ids[b * feat + f], 1) for f in range(feat)]
             lo = [low[a, :] for a in at]
             hi = [high[a, :] for a in at]
             while len(lo) > 1:
@@ -114,10 +149,6 @@
             phigh[pl.ds(b, 1), :] = hi[0]
         return c
 
-    lax.fori_loop(0, users // 8, pool, 0)
-    pooled = jnp.concatenate([plow[...], phigh[...]], axis=1).astype(BF16)
-    group[0] = tower(pooled, u1[...], u2[...])[3].astype(BF16)
-
     far = sorted(range(1, chips), key=lambda k: (min(k, chips - k), k))
     names = [(0, 0), (0, 1)] + [(k, 0) for k in far] + [(k, 1) for k in far]
     slot_of = {name: i for i, name in enumerate(names)}
@@ -129,53 +160,140 @@
             device_id=(to, r), device_id_type=MESH,
         )
 
-    f_copies = {0: push(group.at[0], group.at[1], f_send.at[0], f_recv.at[0], 0, 1)}
-    q_copies = {}
-    for k in far:
-        s = slot_of[(k, 0)]
-        q_copies[k] = push(group.at[0], group.at[s], q_send.at[k], q_recv.at[k], chips - k, 0)
-        f_copies[k] = push(group.at[s], group.at[slot_of[(k, 1)]], f_send.at[k], f_recv.at[k], 0, 1)
-
-    pl.semaphore_wait(barrier, peers - 1)
-    for k in far:
-        q_copies[k].start()
-    f_copies[0].start()
-
-    unit[pl.ds(n, 8), :] = jnp.zeros((8, unit.shape[1]), F32)
-
-    def forward(i, c):
-        at = pl.ds(pl.multiple_of(i * TILE, TILE), TILE)
-        unit[at, :] = tower(table[at, :], w1[...], w2[...])[3]
-        return c
-
-    lax.fori_loop(0, n // TILE, forward, 0)
-
-    def span(t):
-        return pl.ds(pl.multiple_of(t * cap, cap), cap)
-
-    def gather_list(t):
-        for j in range(cap):
-            wide[pl.ds(t * cap + j, 1), :] = unit[pl.ds(rows[j, t], 1), :]
-        send[span(t), :] = wide[span(t), :].astype(BF16)
-
-    def send_list(k, c):
+    quarter = users // PARTS
+
+    def piece(slot, c):
+        return group.at[slot, pl.ds(c * quarter, quarter), :]
+
+    q_copies, f_copies = {}, {}
+    for c in range(PARTS):
+        f_copies[0, c] = push(piece(0, c), piece(1, c), f_send.at[c], f_recv.at[c], 0, 1)
+        for k in far:
+            s, at = slot_of[(k, 0)], k * PARTS + c
+            q_copies[k, c] = push(
+                piece(0, c), piece(s, c), q_send.at[at], q_recv.at[at], chips - k, 0
+            )
+            f_copies[k, c] = push(
+                piece(s, c), piece(slot_of[(k, 1)], c), f_send.at[at], f_recv.at[at], 0, 1
+            )
+
+    def pass_on(c):
+        for k in far:
+            q_copies[k, c].wait_recv()
+            f_copies[k, c].start()
+
+    for c in range(PARTS):
+        at = pl.ds(c * quarter, quarter)
+        lax.fori_loop(c * (quarter // 8), (c + 1) * (quarter // 8), pool, 0)
+        pooled = jnp.concatenate([plow[at, :], phigh[at, :]], axis=1).astype(BF16)
+        group[0, at, :] = tower(pooled, u1[...], u2[...])[3].astype(BF16)
+        for k in far:
+            q_copies[k, c].start()
+        f_copies[0, c].start()
+        if c > 0:
+            pass_on(c - 1)
+
+    keep.wait()
+    others = pl.ds(0, (peers - 1) * cap)
+    pltpu.make_async_copy(send.at[others, :], recv.at[others, :], a_recv).wait()
+    wide[...] = recv[...].astype(F32)
+
+    def pick(i, c):
+        for j in range(32):
+            low[pl.ds(i * 32 + j, 1), :] = wide[pl.ds(neg_slot[i * 32 + j], 1), :]
+        for j in range(32):
+            low[pl.ds(users + i * 32 + j, 1), :] = wide[pl.ds(pos_slot[i * 32 + j], 1), :]
+        return c
+
+    lax.fori_loop(0, users // 32, pick, 0)
+    cols[...] = low[pl.ds(0, 2 * users), :].astype(BF16)
+
+    pass_on(PARTS - 1)
+    s = mm_t(cols[pl.ds(0, users), :], group[0])
+    e = jnp.exp2(s * (LOGIT_SCALE * LOG2E))
+    nexp[...] = e.astype(BF16)
+    neg_sum = jnp.sum(e, axis=0, keepdims=True)
+    s_copies = []
+
+    def compute(first, last):
+        def one(k, c):
+            s = mm_t(cols[pl.ds(users, users), :], group[k])
+            e = jnp.exp2(s * (LOGIT_SCALE * LOG2E))
+            pexp[k] = e.astype(BF16)
+            sums_out[k] = jnp.sum(e, axis=0, keepdims=True)
+            return c
+
+        lax.fori_loop(first, last, one, 0)
+        for i in range(first, last):
+            k, flip = names[i]
+            b = slot_of[((chips - k) % chips, flip)]
+            s_copies.append(push(sums_out.at[i], sums_in.at[b], s_send.at[i], s_recv.at[b], k, flip))
+            s_copies[-1].start()
+
+    for c in f_copies.values():
+        c.wait_recv()
+    compute(1, 5)
+    compute(5, grp)
+
+    s = mm_t(cols[pl.ds(users, users), :], group[0])
+    hit = lax.broadcasted_iota(jnp.int32, s.shape, 0) == lax.broadcasted_iota(jnp.int32, s.shape, 1)
+    e = jnp.where(hit, 0.0, jnp.exp2(s * (LOGIT_SCALE * LOG2E)))
+    own_score = jnp.sum(jnp.where(hit, s, 0.0), axis=0, keepdims=True) * LOGIT_SCALE
+    pexp[0] = e.astype(BF16)
+    other = neg_sum + jnp.sum(e, axis=0, keepdims=True)
+
+    for c in s_copies:
+        c.wait_recv()
+
+    for k in range(1, grp):
+        other = other + sums_in[k]
+    total = other + jnp.exp2(own_score * LOG2E)
+    loss[...] = jnp.log(total) - own_score
+    rate = LOGIT_SCALE / total
+    rates[0] = rate
+    r_copies = []
+    for i in range(1, grp):
+        k, flip = names[i]
+        b = slot_of[((chips - k) % chips, flip)]
+        r_copies.append(push(rates.at[0], rates.at[b], r_send.at[i], r_recv.at[b], k, flip))
+        r_copies[-1].start()
+
+    scaled[0] = (group[0].astype(F32) * upright(rate)).astype(BF16)
+    acc[...] = spread(neg_at[...], mm(nexp[...], scaled[0]))
+    own = group[0].astype(F32) * upright(rate * other)
+    for c in r_copies:
+        c.wait_recv()
+
+    def scale(k, c):
+        scaled[k] = (group[k].astype(F32) * upright(rates[k])).astype(BF16)
+        return c
+
+    lax.fori_loop(1, grp, scale, 0)
+    grads = mm(pexp[0], scaled[0]) - own
+    for k in range(1, grp):
+        grads = grads + mm(pexp[k], scaled[k])
+    total_grads = acc[...] + spread(pos_at[...], grads)
+    half = n // 2
+    back_send[pl.ds(0, half), :] = total_grads[:, :128].astype(BF16)
+    back_send[pl.ds(half, half), :] = total_grads[:, 128:].astype(BF16)
+
+    per = peers // GROUPS
+
+    def send_back(k, c):
         t = lax.rem(me + k, peers)
-        gather_list(t)
         pltpu.make_async_remote_copy(
-            src_ref=send.at[span(t), :], dst_ref=recv.at[span(me), :],
-            send_sem=a_send, recv_sem=a_recv, device_id=place(t), device_id_type=MESH,
+            src_ref=back_send.at[span(t), :], dst_ref=back_recv.at[span(me), :],
+            send_sem=b_send, recv_sem=b_recv.at[me // per], device_id=place(t), device_id_type=MESH,
         ).start()
         return c
 
-    index.wait()
-    lax.fori_loop(1, peers, send_list, 0)
-    gather_list(me)
-    keep = pltpu.make_async_copy(send.at[span(me), :], recv.at[span(me), :], l_sem)
+    lax.fori_loop(1, peers, send_back, 0)
+    keep = pltpu.make_async_copy(
+        back_send.at[span(me), :], back_recv.at[span(me), :], b_recv.at[me // per]
+    )
     keep.start()
-    for k in far:
-        q_copies[k].wait_recv()
-        f_copies[k].start()
-
+
+    o_copies = []
     for i in range(n // TILE):
         at = pl.ds(i * TILE, TILE)
         pre, sig, inv, _ = tower(table[at, :], w1[...], w2[...])
@@ -202,107 +320,6 @@
         part = along[b * (peers // GROUPS):(b + 1) * (peers // GROUPS), :]
         row_at[b:b + 1, :] = jnp.sum(part, axis=0, keepdims=True).astype(jnp.int32)
 
-    keep.wait()
-    others = pl.ds(0, (peers - 1) * cap)
-    pltpu.make_async_copy(send.at[others, :], recv.at[others, :], a_recv).wait()
-    wide[...] = recv[...].astype(F32)
-
-    def pick(i, c):
-        for j in range(32):
-            low[pl.ds(i * 32 + j, 1), :] = wide[pl.ds(neg_slot[i * 32 + j], 1), :]
-        for j in range(32):
-            low[pl.ds(users + i * 32 + j, 1), :] = wide[pl.ds(pos_slot[i * 32 + j], 1), :]
-        return c
-
-    lax.fori_loop(0, users // 32, pick, 0)
-    cols[...] = low[pl.ds(0, 2 * users), :].astype(BF16)
-
-    for c in o_copies:
-        c.wait()
-    s_copies = []
-
-    def compute(first, last):
-        def one(k, c):
-            s = mm_t(cols[pl.ds(users, users), :], group[k])
-            e = jnp.exp2(s * (LOGIT_SCALE * LOG2E))
-            pexp[k] = e.astype(BF16)
-            sums_out[k] = jnp.sum(e, axis=0, keepdims=True)
-            return c
-
-        lax.fori_loop(first, last, one, 0)
-        for i in range(first, last):
-            k, flip = names[i]
-            b = slot_of[((chips - k) % chips, flip)]
-            s_copies.append(push(sums_out.at[i], sums_in.at[b], s_send.at[i], s_recv.at[b], k, flip))
-            s_copies[-1].start()
-
-    for c in f_copies.values():
-        c.wait_recv()
-    compute(1, 5)
-    compute(5, grp)
-
-    s = mm_t(cols[pl.ds(0, users), :], group[0])
-    e = jnp.exp2(s * (LOGIT_SCALE * LOG2E))
-    nexp[...] = e.astype(BF16)
-    other = jnp.sum(e, axis=0, keepdims=True)
-    s = mm_t(cols[pl.ds(users, users), :], group[0])
-    hit = lax.broadcasted_iota(jnp.int32, s.shape, 0) == lax.broadcasted_iota(jnp.int32, s.shape, 1)
-    e = jnp.where(hit, 0.0, jnp.exp2(s * (LOGIT_SCALE * LOG2E)))
-    own_score = jnp.sum(jnp.where(hit, s, 0.0), axis=0, keepdims=True) * LOGIT_SCALE
-    pexp[0] = e.astype(BF16)
-    other = other + jnp.sum(e, axis=0, keepdims=True)
-
-    for c in s_copies:
-        c.wait_recv()
-
-    for k in range(1, grp):
-        other = other + sums_in[k]
-    total = other + jnp.exp2(own_score * LOG2E)
-    loss[...] = jnp.log(total) - own_score
-    rate = LOGIT_SCALE / total
-    rates[0] = rate
-    r_copies = []
-    for i in range(1, grp):
-        k, flip = names[i]
-        b = slot_of[((chips - k) % chips, flip)]
-        r_copies.append(push(rates.at[0], rates.at[b], r_send.at[i], r_recv.at[b], k, flip))
-        r_copies[-1].start()
-
-    scaled[0] = (group[0].astype(F32) * upright(rate)).astype(BF16)
-    acc[...] = spread(neg_at[...], mm(nexp[...], scaled[0]))
-    own = group[0].astype(F32) * upright(rate * other)
-    for c in r_copies:
-        c.wait_recv()
-
-    def scale(k, c):
-        scaled[k] = (group[k].astype(F32) * upright(rates[k])).astype(BF16)
-        return c
-
-    lax.fori_loop(1, grp, scale, 0)
-    grads = mm(pexp[0], scaled[0]) - own
-    for k in range(1, grp):
-        grads = grads + mm(pexp[k], scaled[k])
-    total_grads = acc[...] + spread(pos_at[...], grads)
-    half = n // 2
-    back_send[pl.ds(0, half), :] = total_grads[:, :128].astype(BF16)
-    back_send[pl.ds(half, half), :] = total_grads[:, 128:].astype(BF16)
-
-    per = peers // GROUPS
-
-    def send_back(k, c):
-        t = lax.rem(me + k, peers)
-        pltpu.make_async_remote_copy(
-            src_ref=back_send.at[span(t), :], dst_ref=back_recv.at[span(me), :],
-            send_sem=b_send, recv_sem=b_recv.at[me // per], device_id=place(t), device_id_type=MESH,
-        ).start()
-        return c
-
-    lax.fori_loop(1, peers, send_back, 0)
-    keep = pltpu.make_async_copy(
-        back_send.at[span(me), :], back_recv.at[span(me), :], b_recv.at[me // per]
-    )
-    keep.start()
-
     acc[...] = jnp.zeros(acc.shape, F32)
 
     def arrive(i, c):
@@ -325,6 +342,8 @@
         c.wait_send()
     pltpu.make_async_copy(send.at[others, :], recv.at[others, :], a_send).wait()
     pltpu.make_async_copy(back_send.at[others, :], back_recv.at[others, :], b_send).wait()
+    for c in o_copies:
+        c.wait()
 
 
 def row_kernel(d_out, slopes, w1, w2, out):
@@ -369,7 +388,7 @@
             vm((cap, peers), jnp.int32), pltpu.SMEM((cap, peers), jnp.int32),
             vm((GROUPS, slots // GROUPS), jnp.int32),
             dma, dma, dma((n // TILE,)), dma, dma, dma, dma((GROUPS,)), dma,
-            dma((chips,)), dma((chips,)), dma((chips,)), dma((chips,)),
+            dma((chips * PARTS,)), dma((chips * PARTS,)), dma((chips * PARTS,)), dma((chips * PARTS,)),
             dma((grp,)), dma((grp,)), dma((grp,)), dma((grp,)),
         ],
         compiler_params=pltpu.CompilerParams(
@@ -378,10 +397,10 @@
         cost_estimate=pl.CostEstimate(flops=2**34, bytes_accessed=2**24, transcendentals=2**24),
         name="window",
     )(
-        pos_slot, neg, user_ids.T, send_rows[0].T, send_count, item_table, item_w1, item_w2,
+        pos_slot, neg, user_ids.reshape(-1), send_rows[0].T, send_count, item_table, item_w1, item_w2,
         user_w1, user_w2, pos_slot.reshape(1, -1), neg_slot, user_table,
     )
-    block = 512
+    block = 1024
     table_grad = pl.pallas_call(
         row_kernel,
         out_shape=jax.ShapeDtypeStruct(item_table.shape, F32),
@@ -393,7 +412,7 @@
             pl.BlockSpec(item_w2.shape, lambda i: (0, 0)),
         ],
         out_specs=pl.BlockSpec((block, item_table.shape[1]), lambda i: (i, 0)),
-        compiler_params=pltpu.CompilerParams(vmem_limit_bytes=32 * 2**20),
+        compiler_params=pltpu.CompilerParams(vmem_limit_bytes=60 * 2**20),
         name="row_grads",
     )(d_out, slopes, item_w1, item_w2)
     return table_grad, loss.reshape(-1)

time: 110 us -> 101 us (0.918)
  Pallas kernels: 105 us -> 98.1 us
  local copies, waits for them, and re-layouts: 4.01 us -> 2.4 us
    pallas_call x1, Pallas kernels: 99.4 us -> 91.7 us  [per_device(): pl.pallas_call(window_kernel, out_shape=[jax.ShapeDtypeStruct((n, outw),...]
    unnamed x11 -> x4, local copies, waits for them, and re-layouts: 4.01 us -> 1.55 us
where the time goes in v5:
time: 101 us
  Pallas kernels  98.1 us (97%)
  local copies, waits for them, and re-layouts  2.4 us (2%)
    pallas_call x1, Pallas kernels, per_device(): pl.pallas_call(window_kernel, out_shape=[jax.ShapeDtypeStruct((n, outw),...  91.7 us
    pallas_call x1, Pallas kernels, per_device(): pl.pallas_call(row_kernel, out_shape=jax.ShapeDtypeStruct(item_table.shap...  6.36 us

profile of v5, /device:TPU:1, one launch (start us, length us, event | category | flops | bytes accessed | tf_op | source)
XLA Modules:
  0.0 101.1 jit_solution(3895157882391415652)
XLA Ops:
  0.6 1.0 copy.13
  1.6 0.9 reshape.17.ids
  2.4 91.7 %window.1 = (bf16[4096,128]{1,0:T(8,128)(2,1)}, bf16[4096,512]{1,0:T(8,128)(2,1)}, f32[1,1024]{1,0:T(1,128)}) custom-call(s32[1024]{0:T(1024)} %pos_slot.1, s32[1024]{0:T(1024)} %bitcast.9, s32[8192]{0:T(1024)} %reshape.17.ids, s32[32,128]{1,0:T(8,128)} %bitcast.7, s32[1,128]{1,0:T(1,128)} %counts.1, bf16[4096,256]{1,0:T(8,128)(2,1)} %table.1, ...), custom_call_target="tpu_custom_call" | custom-call | flops 17179869184 | bytes 16777216 | tf_op jit(solution)/shard_map/window/pallas_call | solution.py:368
  94.1 0.0 copy-start
  94.2 6.4 %row_grads.1 = f32[4096,256]{1,0:T(8,128)} custom-call(bf16[4096,128]{1,0:T(8,128)(2,1)} %get-tuple-element.5.d_out, bf16[4096,512]{1,0:T(8,128)(2,1)} %get-tuple-element.6.slopes, bf16[256,512]{1,0:T(8,128)(2,1)} %w1.3, bf16[512,128]{1,0:T(8,128)(2,1)} %w2.3), custom_call_target="tpu_custom_call" | custom-call | tf_op jit(solution)/shard_map/row_grads/pallas_call | solution.py:404
  100.5 0.0 copy-done
  100.5 0.6 copy.15
Async XLA Ops:
  94.1 6.4 %copy-start = (f32[1,1024]{1,0:T(1,128)S(1)}, f32[1,1024]{1,0:T(1,128)}, u32[]{:S(2)}) copy-start(f32[1,1024]{1,0:T(1,128)} %get-tuple-element.7) | copy-start | bytes 12292

commit v6 on v5

v6 whole, which is shorter than its diff:
```python
import math

import jax
import jax.numpy as jnp
from jax import lax
from jax.experimental import pallas as pl
from jax.experimental.pallas import tpu as pltpu
from jax.sharding import PartitionSpec as P

LOGIT_SCALE = 20.0
NORM_EPS = 1e-06
LOG2E = math.log2(math.e)
MESH = pl.DeviceIdType.MESH
VMEM = pl.BlockSpec(memory_space=pltpu.VMEM)
SMEM = pl.BlockSpec(memory_space=pltpu.SMEM)
ANY = pl.BlockSpec(memory_space=pl.ANY)
F32, BF16 = jnp.float32, jnp.bfloat16
TILE = 1024
GROUPS = 8
PARTS = 4


def mm(a, b):
    return jnp.dot(a, b, preferred_element_type=F32)


def mm_t(a, b):
    return lax.dot_general(a, b, (((1,), (1,)), ((), ())), preferred_element_type=F32)


def tower(x, w1, w2):
    pre = mm(x, w1)
    sig = 0.5 + 0.5 * jnp.tanh(0.5 * pre)
    out = mm((pre * sig).astype(BF16), w2)
    inv = lax.rsqrt(jnp.sum(out * out, axis=-1, keepdims=True) + NORM_EPS)
    return pre, sig, inv, out * inv


def upright(row):
    return jnp.transpose(jnp.broadcast_to(row, (128, row.shape[1])))


def spread(at, grads):
    half = 2048
    low = jnp.where(at >= half, at - half, at)
    hot = jnp.where(
        lax.broadcasted_iota(jnp.int32, (half, at.shape[1]), 0) == low, 1.0, 0.0
    ).astype(BF16)
    upper = upright(at.astype(F32)) >= half
    grads = grads.astype(F32)
    both = jnp.concatenate(
        [jnp.where(upper, 0.0, grads), jnp.where(upper, grads, 0.0)], axis=1
    ).astype(BF16)
    return mm(hot, both)


def window_kernel(
    pos_slot, neg_slot, lists, id_rows, counts, table, w1, w2, u1, u2, pos_at, neg_at, user_table,
    d_out, slopes, loss,
    ut, low, high, plow, phigh, unit, wide, send, recv, cols, group, pexp, nexp, scaled,
    sums_out, sums_in, rates, acc, back_send, back_recv, live_rows, rows, row_at,
    ids, t_sem, i_sem, u_sem, o_sem, a_send, a_recv, b_send, b_recv, l_sem,
    q_send, q_recv, f_send, f_recv, s_send, s_recv, r_send, r_recv,
):
    n, users = table.shape[0], group.shape[1]
    cap = 32
    grp, rep = lax.axis_size("grp"), lax.axis_size("rep")
    peers = grp * rep
    chips = grp // 2
    g, r = lax.axis_index("grp"), lax.axis_index("rep")
    me = g * rep + r
    chip, core = g // 2, lax.rem(g, 2)

    def place(t):
        return (t // rep, lax.rem(t, rep))

    barrier = pltpu.get_barrier_semaphore()

    def greet(k, c):
        pl.semaphore_signal(
            barrier, inc=1, device_id=place(lax.rem(me + k, peers)), device_id_type=MESH
        )
        return c

    lax.fori_loop(1, peers, greet, 0)
    fetch = pltpu.make_async_copy(user_table, ut, t_sem)
    fetch.start()

    live = lax.broadcasted_iota(jnp.int32, lists.shape, 0) < counts[...]
    live_rows[...] = jnp.where(live, lists[...], n)
    index = pltpu.make_async_copy(live_rows, rows, i_sem)
    index.start()
    feat = id_rows.shape[0]
    u_copies = [
        pltpu.make_async_copy(id_rows.at[f], ids.at[pl.ds(f * users, users)], u_sem.at[f])
        for f in range(feat)
    ]
    for c in u_copies:
        c.start()

    unit[pl.ds(n, 8), :] = jnp.zeros((8, unit.shape[1]), F32)

    o_copies = []
    for i in range(n // TILE):
        at = pl.ds(i * TILE, TILE)
        pre, sig, inv, unit[at, :] = tower(table[at, :], w1[...], w2[...])
        pexp[i, :, :512] = (sig * (1.0 + pre * (1.0 - sig)) * inv).astype(BF16)
        o_copies.append(
            pltpu.make_async_copy(pexp.at[i, :, pl.ds(0, 512)], slopes.at[at, :], o_sem.at[i])
        )
        o_copies[-1].start()

    low_part = jnp.transpose(live_rows[...].astype(F32))
    high_part = jnp.floor(low_part * (1.0 / 64.0))
    low_part = low_part - 64.0 * high_part
    width = peers // GROUPS * cap
    tiled = (
        lax.broadcasted_iota(jnp.int32, (cap, width), 0)
        == lax.rem(lax.broadcasted_iota(jnp.int32, (cap, width), 1), cap)
    ).astype(F32).astype(BF16)
    along = 64.0 * mm(high_part.astype(BF16), tiled) + mm(low_part.astype(BF16), tiled)
    mine = lax.rem(
        lax.broadcasted_iota(jnp.int32, along.shape, 0), peers // GROUPS
    ) == lax.broadcasted_iota(jnp.int32, along.shape, 1) // cap
    along = jnp.where(mine, along, 0.0)
    for b in range(GROUPS):
        part = along[b * (peers // GROUPS):(b + 1) * (peers // GROUPS), :]
        row_at[b:b + 1, :] = jnp.sum(part, axis=0, keepdims=True).astype(jnp.int32)


    fetch.wait()

    def widen(i, c):
        at = pl.ds(pl.multiple_of(i * 256, 256), 256)
        low[at, :] = ut[at, :128].astype(F32)
        high[at, :] = ut[at, 128:].astype(F32)
        return c

    lax.fori_loop(0, ut.shape[0] // 256, widen, 0)
    pl.semaphore_wait(barrier, peers - 1)

    def span(t):
        return pl.ds(pl.multiple_of(t * cap, cap), cap)

    def gather_list(t):
        for j in range(cap):
            wide[pl.ds(t * cap + j, 1), :] = unit[pl.ds(rows[j, t], 1), :]
        send[span(t), :] = wide[span(t), :].astype(BF16)

    def send_list(k, c):
        t = lax.rem(me + k, peers)
        gather_list(t)
        pltpu.make_async_remote_copy(
            src_ref=send.at[span(t), :], dst_ref=recv.at[span(me), :],
            send_sem=a_send, recv_sem=a_recv, device_id=place(t), device_id_type=MESH,
        ).start()
        return c

    index.wait()
    lax.fori_loop(1, peers, send_list, 0)
    gather_list(me)
    keep = pltpu.make_async_copy(send.at[span(me), :], recv.at[span(me), :], l_sem)
    keep.start()

    for c in u_copies:
        c.wait()

    def pool(i, c):
        for k in range(8):
            b = i * 8 + k
            at = [pl.ds(ids[f * users + b], 1) for f in range(feat)]
            lo = [low[a, :] for a in at]
            hi = [high[a, :] for a in at]
            while len(lo) > 1:
                lo = [x + y for x, y in zip(lo[::2], lo[1::2])]
                hi = [x + y for x, y in zip(hi[::2], hi[1::2])]
            plow[pl.ds(b, 1), :] = lo[0]
            phigh[pl.ds(b, 1), :] = hi[0]
        return c

    far = sorted(range(1, chips), key=lambda k: (min(k, chips - k), k))
    names = [(0, 0), (0, 1)] + [(k, 0) for k in far] + [(k, 1) for k in far]
    slot_of = {name: i for i, name in enumerate(names)}

    def push(src, dst, ss, rs, k, flip):
        to = lax.rem(chip + k, chips) * 2 + (1 - core if flip else core)
        return pltpu.make_async_remote_copy(
            src_ref=src, dst_ref=dst, send_sem=ss, recv_sem=rs,
            device_id=(to, r), device_id_type=MESH,
        )

    quarter = users // PARTS

    def piece(slot, c):
        return group.at[slot, pl.ds(c * quarter, quarter), :]

    middle = 2 if chips == 4 else 0
    near = [k for k in far if k != middle]
    q_copies, f_copies = {}, {}
    for c in range(PARTS):
        f_copies[0, c] = push(piece(0, c), piece(1, c), f_send.at[c], f_recv.at[c], 0, 1)
        for k in far:
            s, at = slot_of[(k, 0)], k * PARTS + c
            src, to = 0, chips - k
            if k == middle:
                src, to = (slot_of[(1, 0)], chips - 1) if c % 2 == 0 else (slot_of[(chips - 1, 0)], 1)
            q_copies[k, c] = push(piece(src, c), piece(s, c), q_send.at[at], q_recv.at[at], to, 0)
            f_copies[k, c] = push(
                piece(s, c), piece(slot_of[(k, 1)], c), f_send.at[at], f_recv.at[at], 0, 1
            )

    def near_on(c):
        for k in near:
            q_copies[k, c].wait_recv()
            f_copies[k, c].start()
        if middle:
            q_copies[middle, c].start()

    def far_on(c):
        if middle:
            q_copies[middle, c].wait_recv()
            f_copies[middle, c].start()

    for c in range(PARTS):
        at = pl.ds(c * quarter, quarter)
        lax.fori_loop(c * (quarter // 8), (c + 1) * (quarter // 8), pool, 0)
        pooled = jnp.concatenate([plow[at, :], phigh[at, :]], axis=1).astype(BF16)
        group[0, at, :] = tower(pooled, u1[...], u2[...])[3].astype(BF16)
        for k in near:
            q_copies[k, c].start()
        f_copies[0, c].start()
        if c > 0:
            near_on(c - 1)
        if c > 1:
            far_on(c - 2)
    near_on(PARTS - 1)
    far_on(PARTS - 2)

    keep.wait()
    others = pl.ds(0, (peers - 1) * cap)
    pltpu.make_async_copy(send.at[others, :], recv.at[others, :], a_recv).wait()
    wide[...] = recv[...].astype(F32)

    def pick(i, c):
        for j in range(32):
            low[pl.ds(i * 32 + j, 1), :] = wide[pl.ds(neg_slot[i * 32 + j], 1), :]
        for j in range(32):
            low[pl.ds(users + i * 32 + j, 1), :] = wide[pl.ds(pos_slot[i * 32 + j], 1), :]
        return c

    lax.fori_loop(0, users // 32, pick, 0)
    cols[...] = low[pl.ds(0, 2 * users), :].astype(BF16)

    far_on(PARTS - 1)
    for c in o_copies:
        c.wait()
    s = mm_t(cols[pl.ds(0, users), :], group[0])
    e = jnp.exp2(s * (LOGIT_SCALE * LOG2E))
    nexp[...] = e.astype(BF16)
    neg_sum = jnp.sum(e, axis=0, keepdims=True)
    s_copies = []

    def compute(first, last):
        def one(k, c):
            s = mm_t(cols[pl.ds(users, users), :], group[k])
            e = jnp.exp2(s * (LOGIT_SCALE * LOG2E))
            pexp[k] = e.astype(BF16)
            sums_out[k] = jnp.sum(e, axis=0, keepdims=True)
            return c

        lax.fori_loop(first, last, one, 0)
        for i in range(first, last):
            k, flip = names[i]
            b = slot_of[((chips - k) % chips, flip)]
            s_copies.append(push(sums_out.at[i], sums_in.at[b], s_send.at[i], s_recv.at[b], k, flip))
            s_copies[-1].start()

    for c in f_copies.values():
        c.wait_recv()
    compute(1, 5)
    compute(5, grp)

    s = mm_t(cols[pl.ds(users, users), :], group[0])
    hit = lax.broadcasted_iota(jnp.int32, s.shape, 0) == lax.broadcasted_iota(jnp.int32, s.shape, 1)
    e = jnp.where(hit, 0.0, jnp.exp2(s * (LOGIT_SCALE * LOG2E)))
    own_score = jnp.sum(jnp.where(hit, s, 0.0), axis=0, keepdims=True) * LOGIT_SCALE
    pexp[0] = e.astype(BF16)
    other = neg_sum + jnp.sum(e, axis=0, keepdims=True)

    for c in s_copies:
        c.wait_recv()

    for k in range(1, grp):
        other = other + sums_in[k]
    total = other + jnp.exp2(own_score * LOG2E)
    loss[...] = jnp.log(total) - own_score
    rate = LOGIT_SCALE / total
    rates[0] = rate
    r_copies = []
    for i in range(1, grp):
        k, flip = names[i]
        b = slot_of[((chips - k) % chips, flip)]
        r_copies.append(push(rates.at[0], rates.at[b], r_send.at[i], r_recv.at[b], k, flip))
        r_copies[-1].start()

    scaled[0] = (group[0].astype(F32) * upright(rate)).astype(BF16)
    acc[...] = spread(neg_at[...], mm(nexp[...], scaled[0]))
    own = group[0].astype(F32) * upright(rate * other)
    for c in r_copies:
        c.wait_recv()

    def scale(k, c):
        scaled[k] = (group[k].astype(F32) * upright(rates[k])).astype(BF16)
        return c

    lax.fori_loop(1, grp, scale, 0)
    grads = mm(pexp[0], scaled[0]) - own
    for k in range(1, grp):
        grads = grads + mm(pexp[k], scaled[k])
    total_grads = acc[...] + spread(pos_at[...], grads)
    half = n // 2
    back_send[pl.ds(0, half), :] = total_grads[:, :128].astype(BF16)
    back_send[pl.ds(half, half), :] = total_grads[:, 128:].astype(BF16)

    per = peers // GROUPS

    def send_back(k, c):
        t = lax.rem(me + k, peers)
        pltpu.make_async_remote_copy(
            src_ref=back_send.at[span(t), :], dst_ref=back_recv.at[span(me), :],
            send_sem=b_send, recv_sem=b_recv.at[me // per], device_id=place(t), device_id_type=MESH,
        ).start()
        return c

    lax.fori_loop(1, peers, send_back, 0)
    keep = pltpu.make_async_copy(
        back_send.at[span(me), :], back_recv.at[span(me), :], b_recv.at[me // per]
    )
    keep.start()

    acc[...] = jnp.zeros(acc.shape, F32)

    def arrive(i, c):
        b = lax.rem(me // per + 2 * GROUPS - 1 - i, GROUPS)
        at = pl.ds(pl.multiple_of(b * (per * cap), per * cap), per * cap)
        pltpu.make_async_copy(back_send.at[at, :], back_recv.at[at, :], b_recv.at[b]).wait()
        acc[...] = acc[...] + spread(row_at[pl.ds(b, 1), :], back_recv[at, :])
        return c

    lax.fori_loop(0, GROUPS, arrive, 0)

    for i in range(n // TILE):
        at = pl.ds(i * TILE, TILE)
        side = i * TILE // half * 128
        grad = acc[pl.ds(i * TILE % half, TILE), side:side + 128]
        u = unit[at, :]
        d_out[at, :] = (grad - u * jnp.sum(u * grad, axis=-1, keepdims=True)).astype(BF16)

    for c in list(q_copies.values()) + list(f_copies.values()) + s_copies + r_copies:
        c.wait_send()
    pltpu.make_async_copy(send.at[others, :], recv.at[others, :], a_send).wait()
    pltpu.make_async_copy(back_send.at[others, :], back_recv.at[others, :], b_send).wait()


def row_kernel(d_out, slopes, w1, w2, loss_in, out, loss):
    loss[...] = loss_in[...]
    d_pre = (mm_t(d_out[...], w2[...]) * slopes[...].astype(F32)).astype(BF16)
    out[...] = mm_t(d_pre, w1[...])


def per_device(
    item_table, send_rows, send_count, pos_slot, neg_slot, user_ids,
    user_table, item_w1, item_w2, user_w1, user_w2,
):
    peers, cap = send_rows.shape[1:]
    slots = peers * cap
    n, users = item_table.shape[0], pos_slot.shape[0]
    vocab, outw = user_table.shape[0], item_w2.shape[1]
    grp = lax.axis_size("grp")
    chips = grp // 2
    neg = neg_slot.reshape(-1)

    dma = pltpu.SemaphoreType.DMA
    vm = pltpu.VMEM
    d_out, slopes, loss = pl.pallas_call(
        window_kernel,
        out_shape=[
            jax.ShapeDtypeStruct((n, outw), BF16),
            jax.ShapeDtypeStruct((n, item_w1.shape[1]), BF16),
            jax.ShapeDtypeStruct((1, users), F32),
        ],
        in_specs=[SMEM] * 2 + [VMEM] * 10 + [ANY],
        out_specs=[VMEM, ANY, VMEM],
        scratch_shapes=[
            vm(user_table.shape, BF16), vm((vocab, 128), F32), vm((vocab, 128), F32),
            vm((users, 128), F32), vm((users, 128), F32),
            vm((n + 8, outw), F32), vm((slots, outw), F32),
            vm((slots, outw), BF16), vm((slots, outw), BF16),
            vm((2 * users, outw), BF16),
            vm((grp, users, outw), BF16), vm((grp, users, users), BF16), vm((users, users), BF16),
            vm((grp, users, outw), BF16),
            vm((grp, 1, users), F32), vm((grp, 1, users), F32), vm((grp, 1, users), F32),
            vm((n // 2, 2 * outw), F32),
            vm((slots, outw), BF16), vm((slots, outw), BF16),
            vm((cap, peers), jnp.int32), pltpu.SMEM((cap, peers), jnp.int32),
            vm((GROUPS, slots // GROUPS), jnp.int32),
            pltpu.SMEM((user_ids.size,), jnp.int32),
            dma, dma, dma((user_ids.shape[1],)), dma((n // TILE,)), dma, dma, dma, dma((GROUPS,)), dma,
            dma((chips * PARTS,)), dma((chips * PARTS,)), dma((chips * PARTS,)), dma((chips * PARTS,)),
            dma((grp,)), dma((grp,)), dma((grp,)), dma((grp,)),
        ],
        compiler_params=pltpu.CompilerParams(
            collective_id=0, has_side_effects=True, vmem_limit_bytes=60 * 2**20
        ),
        cost_estimate=pl.CostEstimate(flops=2**34, bytes_accessed=2**24, transcendentals=2**24),
        name="window",
    )(
        pos_slot, neg, send_rows[0].T, user_ids.T, send_count, item_table, item_w1, item_w2,
        user_w1, user_w2, pos_slot.reshape(1, -1), neg_slot, user_table,
    )
    block = 512
    table_grad, loss = pl.pallas_call(
        row_kernel,
        out_shape=[
            jax.ShapeDtypeStruct(item_table.shape, F32),
            jax.ShapeDtypeStruct((1, users), F32),
        ],
        grid=(n // block,),
        in_specs=[
            pl.BlockSpec((block, outw), lambda i: (i, 0)),
            pl.BlockSpec((block, item_w1.shape[1]), lambda i: (i, 0)),
            pl.BlockSpec(item_w1.shape, lambda i: (0, 0)),
            pl.BlockSpec(item_w2.shape, lambda i: (0, 0)),
            pl.BlockSpec((1, users), lambda i: (0, 0)),
        ],
        out_specs=[
            pl.BlockSpec((block, item_table.shape[1]), lambda i: (i, 0)),
            pl.BlockSpec((1, users), lambda i: (0, 0)),
        ],
        compiler_params=pltpu.CompilerParams(vmem_limit_bytes=60 * 2**20),
        name="row_grads",
    )(d_out, slopes, item_w1, item_w2, loss)
    return table_grad, loss.reshape(-1)


def solution(mesh):
    return jax.shard_map(
        per_device,
        mesh=mesh,
        in_specs=(
            P(("grp", "rep"), None),
            P(("grp", "rep"), None, None),
            P(("grp", "rep"), None),
            P(("grp", "rep")),
            P(("grp", "rep"), None),
            P(("grp", "rep"), None),
            P(), P(), P(), P(), P(),
        ),
        out_specs=(P(("grp", "rep"), None), P(("grp", "rep"))),
        check_vma=False,
    )
```

time: 101 us -> 102 us (level)
  Pallas kernels: 98.1 us -> 101 us
  local copies, waits for them, and re-layouts: 2.4 us -> 0 us
    pallas_call x1, Pallas kernels: 6.36 us -> 8.37 us  [per_device(): pl.pallas_call(row_kernel, out_shape=[jax.ShapeDtypeStruct(item_table.sha...]
    unnamed x4 -> x0, local copies, waits for them, and re-layouts: 1.55 us -> none
where the time goes in v6:
time: 102 us
  Pallas kernels  101 us (99%)
    pallas_call x1, Pallas kernels, per_device(): pl.pallas_call(window_kernel, out_shape=[jax.ShapeDtypeStruct((n, outw),...  92.5 us
    pallas_call x1, Pallas kernels, per_device(): pl.pallas_call(row_kernel, out_shape=[jax.ShapeDtypeStruct(item_table.sha...  8.37 us

profile of v6, /device:TPU:1, one launch (start us, length us, event | category | flops | bytes accessed | tf_op | source)
XLA Modules:
  0.0 101.5 jit_solution(16772355953124042103)
XLA Ops:
  0.6 92.5 %window.1 = (bf16[4096,128]{1,0:T(8,128)(2,1)}, bf16[4096,512]{1,0:T(8,128)(2,1)}, f32[1,1024]{1,0:T(1,128)}) custom-call(s32[1024]{0:T(1024)} %pos_slot.1, s32[1024]{0:T(1024)} %bitcast.10, s32[32,128]{1,0:T(8,128)} %bitcast.8, s32[8,1024]{1,0:T(8,128)} %bitcast.7, s32[1,128]{1,0:T(1,128)} %counts.1, bf16[4096,256]{1,0:T(8,128)(2,1)} %table.1, ...), custom_call_target="tpu_custom_call" | custom-call | flops 17179869184 | bytes 16777216 | tf_op jit(solution)/shard_map/window/pallas_call | solution.py:385
  93.1 8.4 %row_grads.1 = (f32[4096,256]{1,0:T(8,128)}, f32[1,1024]{1,0:T(1,128)}) custom-call(bf16[4096,128]{1,0:T(8,128)(2,1)} %get-tuple-element.7.d_out, bf16[4096,512]{1,0:T(8,128)(2,1)} %get-tuple-element.8.slopes, bf16[256,512]{1,0:T(8,128)(2,1)} %w1.3, bf16[512,128]{1,0:T(8,128)(2,1)} %w2.3, f32[1,1024]{1,0:T(1,128)} %get-tuple-element.9.loss_in), custom_call_target="tpu_custom_call" | custom-call | tf_op jit(solution)/shard_map/row_grads/pallas_call | solution.py:422

commit v7 on v6

--- a/solution.py
+++ b/solution.py
@@ -59,7 +59,7 @@
     d_out, slopes, loss,
     ut, low, high, plow, phigh, unit, wide, send, recv, cols, group, pexp, nexp, scaled,
     sums_out, sums_in, rates, acc, back_send, back_recv, live_rows, rows, row_at,
-    ids, t_sem, i_sem, u_sem, o_sem, a_send, a_recv, b_send, b_recv, l_sem,
+    ids, meet, t_sem, i_sem, u_sem, o_sem, a_send, a_recv, b_send, b_recv, l_sem,
     q_send, q_recv, f_send, f_recv, s_send, s_recv, r_send, r_recv,
 ):
     n, users = table.shape[0], group.shape[1]
@@ -76,13 +76,23 @@
 
     barrier = pltpu.get_barrier_semaphore()
 
-    def greet(k, c):
-        pl.semaphore_signal(
-            barrier, inc=1, device_id=place(lax.rem(me + k, peers)), device_id_type=MESH
-        )
-        return c
-
-    lax.fori_loop(1, peers, greet, 0)
+    def greet(sem, to):
+        pl.semaphore_signal(sem, inc=1, device_id=to, device_id_type=MESH)
+
+    def greet_grp(k, c):
+        greet(barrier, (lax.rem(g + k, grp), r))
+        return c
+
+    def greet_rep(k, c):
+        greet(barrier, (g, lax.rem(r + k, rep)))
+        return c
+
+    def greet_again(k, c):
+        greet(meet, (g, lax.rem(r + k, rep)))
+        return c
+
+    lax.fori_loop(1, grp, greet_grp, 0)
+    lax.fori_loop(1, rep, greet_rep, 0)
     fetch = pltpu.make_async_copy(user_table, ut, t_sem)
     fetch.start()
 
@@ -109,6 +119,9 @@
             pltpu.make_async_copy(pexp.at[i, :, pl.ds(0, 512)], slopes.at[at, :], o_sem.at[i])
         )
         o_copies[-1].start()
+
+    pl.semaphore_wait(barrier, grp + rep - 2)
+    lax.fori_loop(1, rep, greet_again, 0)
 
     low_part = jnp.transpose(live_rows[...].astype(F32))
     high_part = jnp.floor(low_part * (1.0 / 64.0))
@@ -137,7 +150,7 @@
         return c
 
     lax.fori_loop(0, ut.shape[0] // 256, widen, 0)
-    pl.semaphore_wait(barrier, peers - 1)
+    pl.semaphore_wait(meet, rep - 1)
 
     def span(t):
         return pl.ds(pl.multiple_of(t * cap, cap), cap)
@@ -404,7 +417,7 @@
             vm((slots, outw), BF16), vm((slots, outw), BF16),
             vm((cap, peers), jnp.int32), pltpu.SMEM((cap, peers), jnp.int32),
             vm((GROUPS, slots // GROUPS), jnp.int32),
-            pltpu.SMEM((user_ids.size,), jnp.int32),
+            pltpu.SMEM((user_ids.size,), jnp.int32), pltpu.SemaphoreType.REGULAR,
             dma, dma, dma((user_ids.shape[1],)), dma((n // TILE,)), dma, dma, dma, dma((GROUPS,)), dma,
             dma((chips * PARTS,)), dma((chips * PARTS,)), dma((chips * PARTS,)), dma((chips * PARTS,)),
             dma((grp,)), dma((grp,)), dma((grp,)), dma((grp,)),
@@ -418,7 +431,7 @@
         pos_slot, neg, send_rows[0].T, user_ids.T, send_count, item_table, item_w1, item_w2,
         user_w1, user_w2, pos_slot.reshape(1, -1), neg_slot, user_table,
     )
-    block = 512
+    block = 1024
     table_grad, loss = pl.pallas_call(
         row_kernel,
         out_shape=[

time: 102 us -> 97.7 us (0.958)
  Pallas kernels: 101 us -> 96.2 us
    pallas_call x1, Pallas kernels: 92.5 us -> 89.8 us  [per_device(): pl.pallas_call(window_kernel, out_shape=[jax.ShapeDtypeStruct((n, outw),...]
    pallas_call x1, Pallas kernels: 8.37 us -> 6.38 us  [per_device(): pl.pallas_call(row_kernel, out_shape=[jax.ShapeDtypeStruct(item_table.sha...]
where the time goes in v7:
time: 97.7 us; the launch traced here: 96.9 us
  Pallas kernels  96.2 us (98%)
    pallas_call x1, Pallas kernels, per_device(): pl.pallas_call(window_kernel, out_shape=[jax.ShapeDtypeStruct((n, outw),...  89.8 us
    pallas_call x1, Pallas kernels, per_device(): pl.pallas_call(row_kernel, out_shape=[jax.ShapeDtypeStruct(item_table.sha...  6.38 us

profile of v7, /device:TPU:1, one launch (start us, length us, event | category | flops | bytes accessed | tf_op | source)
XLA Modules:
  0.0 96.9 jit_solution(3425408045823005741)
XLA Ops:
  0.6 89.8 %window.1 = (bf16[4096,128]{1,0:T(8,128)(2,1)}, bf16[4096,512]{1,0:T(8,128)(2,1)}, f32[1,1024]{1,0:T(1,128)}) custom-call(s32[1024]{0:T(1024)} %pos_slot.1, s32[1024]{0:T(1024)} %bitcast.10, s32[32,128]{1,0:T(8,128)} %bitcast.8, s32[8,1024]{1,0:T(8,128)} %bitcast.7, s32[1,128]{1,0:T(1,128)} %counts.1, bf16[4096,256]{1,0:T(8,128)(2,1)} %table.1, ...), custom_call_target="tpu_custom_call" | custom-call | flops 17179869184 | bytes 16777216 | tf_op jit(solution)/shard_map/window/pallas_call | solution.py:398
  90.5 6.4 %row_grads.1 = (f32[4096,256]{1,0:T(8,128)}, f32[1,1024]{1,0:T(1,128)}) custom-call(bf16[4096,128]{1,0:T(8,128)(2,1)} %get-tuple-element.7.d_out, bf16[4096,512]{1,0:T(8,128)(2,1)} %get-tuple-element.8.slopes, bf16[256,512]{1,0:T(8,128)(2,1)} %w1.3, bf16[512,128]{1,0:T(8,128)(2,1)} %w2.3, f32[1,1024]{1,0:T(1,128)} %get-tuple-element.9.loss_in), custom_call_target="tpu_custom_call" | custom-call | tf_op jit(solution)/shard_map/row_grads/pallas_call | solution.py:435

commit v8 on v7

--- a/solution.py
+++ b/solution.py
@@ -160,17 +160,23 @@
             wide[pl.ds(t * cap + j, 1), :] = unit[pl.ds(rows[j, t], 1), :]
         send[span(t), :] = wide[span(t), :].astype(BF16)
 
-    def send_list(k, c):
-        t = lax.rem(me + k, peers)
-        gather_list(t)
-        pltpu.make_async_remote_copy(
-            src_ref=send.at[span(t), :], dst_ref=recv.at[span(me), :],
-            send_sem=a_send, recv_sem=a_recv, device_id=place(t), device_id_type=MESH,
-        ).start()
+    def send_lists(ks):
+        ts = [lax.rem(me + k, peers) for k in ks]
+        for t in ts:
+            gather_list(t)
+        for t in ts:
+            pltpu.make_async_remote_copy(
+                src_ref=send.at[span(t), :], dst_ref=recv.at[span(me), :],
+                send_sem=a_send, recv_sem=a_recv, device_id=place(t), device_id_type=MESH,
+            ).start()
+
+    def send_pair(i, c):
+        send_lists([2 * i + 1, 2 * i + 2])
         return c
 
     index.wait()
-    lax.fori_loop(1, peers, send_list, 0)
+    lax.fori_loop(0, (peers - 1) // 2, send_pair, 0)
+    send_lists([peers - 1])
     gather_list(me)
     keep = pltpu.make_async_copy(send.at[span(me), :], recv.at[span(me), :], l_sem)
     keep.start()
@@ -179,8 +185,8 @@
         c.wait()
 
     def pool(i, c):
-        for k in range(8):
-            b = i * 8 + k
+        for k in range(16):
+            b = i * 16 + k
             at = [pl.ds(ids[f * users + b], 1) for f in range(feat)]
             lo = [low[a, :] for a in at]
             hi = [high[a, :] for a in at]
@@ -236,7 +242,7 @@
 
     for c in range(PARTS):
         at = pl.ds(c * quarter, quarter)
-        lax.fori_loop(c * (quarter // 8), (c + 1) * (quarter // 8), pool, 0)
+        lax.fori_loop(c * (quarter // 16), (c + 1) * (quarter // 16), pool, 0)
         pooled = jnp.concatenate([plow[at, :], phigh[at, :]], axis=1).astype(BF16)
         group[0, at, :] = tower(pooled, u1[...], u2[...])[3].astype(BF16)
         for k in near:

time: 97.7 us -> 97.4 us (level)
  no operation moved by 1% of the time
where the time goes in v8:
time: 97.4 us; the launch traced here: 96.5 us
  Pallas kernels  95.8 us (98%)
    pallas_call x1, Pallas kernels, per_device(): pl.pallas_call(window_kernel, out_shape=[jax.ShapeDtypeStruct((n, outw),...  89.5 us
    pallas_call x1, Pallas kernels, per_device(): pl.pallas_call(row_kernel, out_shape=[jax.ShapeDtypeStruct(item_table.sha...  6.38 us

profile of v8, /device:TPU:1, one launch (start us, length us, event | category | flops | bytes accessed | tf_op | source)
XLA Modules:
  0.0 96.5 jit_solution(277508487417254288)
XLA Ops:
  0.6 89.5 %window.1 = (bf16[4096,128]{1,0:T(8,128)(2,1)}, bf16[4096,512]{1,0:T(8,128)(2,1)}, f32[1,1024]{1,0:T(1,128)}) custom-call(s32[1024]{0:T(1024)} %pos_slot.1, s32[1024]{0:T(1024)} %bitcast.10, s32[32,128]{1,0:T(8,128)} %bitcast.8, s32[8,1024]{1,0:T(8,128)} %bitcast.7, s32[1,128]{1,0:T(1,128)} %counts.1, bf16[4096,256]{1,0:T(8,128)(2,1)} %table.1, ...), custom_call_target="tpu_custom_call" | custom-call | flops 17179869184 | bytes 16777216 | tf_op jit(solution)/shard_map/window/pallas_call | solution.py:404
  90.1 6.4 %row_grads.1 = (f32[4096,256]{1,0:T(8,128)}, f32[1,1024]{1,0:T(1,128)}) custom-call(bf16[4096,128]{1,0:T(8,128)(2,1)} %get-tuple-element.7.d_out, bf16[4096,512]{1,0:T(8,128)(2,1)} %get-tuple-element.8.slopes, bf16[256,512]{1,0:T(8,128)(2,1)} %w1.3, bf16[512,128]{1,0:T(8,128)(2,1)} %w2.3, f32[1,1024]{1,0:T(1,128)} %get-tuple-element.9.loss_in), custom_call_target="tpu_custom_call" | custom-call | tf_op jit(solution)/shard_map/row_grads/pallas_call | solution.py:441

commit v9 on v7

--- a/solution.py
+++ b/solution.py
@@ -17,7 +17,7 @@
 F32, BF16 = jnp.float32, jnp.bfloat16
 TILE = 1024
 GROUPS = 8
-PARTS = 4
+PARTS = 2
 
 
 def mm(a, b):

time: 97.7 us -> 94.6 us (0.968)
  Pallas kernels: 96.2 us -> 93.1 us
    pallas_call x1, Pallas kernels: 89.8 us -> 86.7 us  [per_device(): pl.pallas_call(window_kernel, out_shape=[jax.ShapeDtypeStruct((n, outw),...]
where the time goes in v9:
time: 94.6 us; the launch traced here: 93.7 us
  Pallas kernels  93.1 us (98%)
    pallas_call x1, Pallas kernels, per_device(): pl.pallas_call(window_kernel, out_shape=[jax.ShapeDtypeStruct((n, outw),...  86.7 us
    pallas_call x1, Pallas kernels, per_device(): pl.pallas_call(row_kernel, out_shape=[jax.ShapeDtypeStruct(item_table.sha...  6.38 us

profile of v9, /device:TPU:1, one launch (start us, length us, event | category | flops | bytes accessed | tf_op | source)
XLA Modules:
  0.0 93.7 jit_solution(4839244713059877938)
XLA Ops:
  0.6 86.7 %window.1 = (bf16[4096,128]{1,0:T(8,128)(2,1)}, bf16[4096,512]{1,0:T(8,128)(2,1)}, f32[1,1024]{1,0:T(1,128)}) custom-call(s32[1024]{0:T(1024)} %pos_slot.1, s32[1024]{0:T(1024)} %bitcast.10, s32[32,128]{1,0:T(8,128)} %bitcast.8, s32[8,1024]{1,0:T(8,128)} %bitcast.7, s32[1,128]{1,0:T(1,128)} %counts.1, bf16[4096,256]{1,0:T(8,128)(2,1)} %table.1, ...), custom_call_target="tpu_custom_call" | custom-call | flops 17179869184 | bytes 16777216 | tf_op jit(solution)/shard_map/window/pallas_call | solution.py:398
  87.3 6.4 %row_grads.1 = (f32[4096,256]{1,0:T(8,128)}, f32[1,1024]{1,0:T(1,128)}) custom-call(bf16[4096,128]{1,0:T(8,128)(2,1)} %get-tuple-element.7.d_out, bf16[4096,512]{1,0:T(8,128)(2,1)} %get-tuple-element.8.slopes, bf16[256,512]{1,0:T(8,128)(2,1)} %w1.3, bf16[512,128]{1,0:T(8,128)(2,1)} %w2.3, f32[1,1024]{1,0:T(1,128)} %get-tuple-element.9.loss_in), custom_call_target="tpu_custom_call" | custom-call | tf_op jit(solution)/shard_map/row_grads/pallas_call | solution.py:435
